TPU v7x, 32 devices: a whole 2x2x4 slice. The times are simulated.
32 devices in a mesh: parts: 2 (over y), dp: 4 (over z), tensor: 2 (over x), sub: 2 (over core).
Axes of the slice: x: 2, y: 2, z: 4, core: 2. Of those that a mesh axis runs over, the one named last changes fastest.
Arguments:
- layer_normed_input: bfloat16 [8192, 8192], P(('parts', 'dp'), ('tensor', 'sub')), parts along dimension 0, may hold values from -6 to 6
- value_gradient: bfloat16 [8192, 1024], P(('parts', 'dp'), ('tensor', 'sub')), parts along dimension 0, may hold values from -6 to 6
- value_matrix: bfloat16 [8192, 1024], P(None, ('tensor', 'sub')), may hold values from -0.1875 to 0.1875
- adapter_down_table: bfloat16 [8, 16, 8192], P(('parts', 'dp'), None, ('tensor', 'sub')), parts along dimension 0, may hold values from -0.0625 to 0.0625
- adapter_up_table: bfloat16 [8, 16, 1024], P(('parts', 'dp'), None, ('tensor', 'sub')), parts along dimension 0, may hold values from -0.1875 to 0.1875
- live_token_count: int32 [8], P('parts'), parts along dimension 0, may hold values from 1 to 1920, as said below
- block_customer: int32 [64], P(('parts', 'dp')), parts along dimension 0, may hold values from 0 to 3, as said below
- customer_slot: int32 [8], P('parts'), parts along dimension 0, may hold values from 0 to 3, as said below
- dropout_flags: int32 [4096], P(('parts', 'dp')), parts along dimension 0, may hold values from -2147483648 to 2147483646
Outputs:
- input_grad: bfloat16 [8192, 8192], P(('parts', 'dp'), ('tensor', 'sub')), parts along dimension 0
- down_grad: float32 [8, 16, 8192], P(('parts', 'dp'), None, ('tensor', 'sub')), parts along dimension 0
- up_grad: float32 [8, 16, 1024], P(('parts', 'dp'), None, ('tensor', 'sub')), parts along dimension 0
There are 2 independent parts, one for each index of `parts`. A program takes and returns all parts, laid end to end along the dimension named above; an argument that names none is the same for every part. Nothing has to cross between parts.
Inputs may be any that keep to these rules, and one draw needn't show every extreme that they name: `live_token_count`: the blocks of one tenant are consecutive; a tenant with c live tokens has exactly ceil(c / 128) blocks, so each tenant has one or more. `block_customer`: blocks of one tenant are consecutive and every tenant has a block. Each slot once; the adapters and the gradients of tenant t sit in row customer_slot[t].
All inputs are finite; a program needn't handle non-finite values.
Results may differ from a plain program's by a relative error of at most 0.012.
Values may be sent and summed in bfloat16 or wider, within the bound.
A program may use at most 128 MiB of HBM per device.

v0:
```python
import jax
import jax.numpy as jnp
from jax import lax
from jax.sharding import PartitionSpec as P

ADAPTER_RANK = 16
BLOCK = 128


adapter_scale = 2.0


def entering(array, axis, combine, identity):
    count, place = (lax.axis_size(axis), lax.axis_index(axis))
    everything = lax.all_gather(array, axis)
    start = jnp.broadcast_to(jnp.asarray(identity, array.dtype), array.shape)

    def turn(k, before):
        reached = k < place
        new = combine(before, everything[k])
        return jnp.where(reached, new, before)

    return lax.fori_loop(0, count, turn, start)


def add_counts(earlier_part, later_part):
    return earlier_part + later_part


def unpack_drop(words):
    shifts = jnp.arange(32, dtype=jnp.int32)
    bits_all = jnp.bitwise_and(jnp.right_shift(words[:, None], shifts[None, :]), 1)
    return (2.0 * bits_all.astype(jnp.float32)).reshape(words.shape[0] * 2, ADAPTER_RANK)


def body(
    layer_normed_input,
    value_gradient,
    value_matrix,
    adapter_down_table,
    adapter_up_table,
    live_token_count,
    block_customer,
    customer_slot,
    dropout_flags,
):
    tenants = live_token_count.shape[0]
    blocks = block_customer.shape[0]
    tok_rows = layer_normed_input.shape[0]
    width_local = layer_normed_input.shape[1]
    value_local = value_gradient.shape[1]
    local_slots = adapter_down_table.shape[0]
    tenant_ids = jnp.arange(tenants, dtype=jnp.int32)
    onehot = (block_customer[:, None] == tenant_ids[None, :]).astype(jnp.int32)
    before = entering(jnp.sum(onehot, 0), "dp", add_counts, jnp.zeros((tenants,), jnp.int32))
    earlier = jnp.cumsum(onehot, 0) - onehot + before[None, :]
    segment_index = jnp.sum(onehot * earlier, 1)
    tenant_count = jnp.sum(onehot * live_token_count[None, :], 1)
    live_rows = jnp.clip(tenant_count - BLOCK * segment_index, 0, BLOCK)
    keep_rows = (jnp.arange(BLOCK, dtype=jnp.int32)[None, :] < live_rows[:, None]).reshape(tok_rows)
    grad_kept = jnp.where(keep_rows[:, None], value_gradient, jnp.zeros_like(value_gradient))
    dropout_keep = unpack_drop(dropout_flags).reshape(blocks, BLOCK, ADAPTER_RANK)
    slot_block = jnp.sum(onehot * customer_slot[None, :], 1)
    select = slot_block[:, None] == tenant_ids[None, :]
    table_down, table_up = (
        lax.all_gather(adapter_down_table, "dp", axis=0, tiled=True),
        lax.all_gather(adapter_up_table, "dp", axis=0, tiled=True),
    )
    select_half = select.astype(jnp.bfloat16)
    block_down_lookup = jnp.einsum(
        "bs,srd->brd", select_half, table_down, preferred_element_type=jnp.float32
    ).astype(jnp.bfloat16)
    up_block_map = jnp.einsum(
        "bs,src->brc", select_half, table_up, preferred_element_type=jnp.float32
    ).astype(jnp.bfloat16)
    input_token_rows = layer_normed_input.reshape(blocks, BLOCK, width_local)
    grad_rows = grad_kept.reshape(blocks, BLOCK, value_local)
    input_part = jnp.einsum(
        "xzu,xtu->xzt", input_token_rows, block_down_lookup, preferred_element_type=jnp.float32
    )
    grad_part = jnp.einsum(
        "bkc,brc->bkr", grad_rows, up_block_map, preferred_element_type=jnp.float32
    )
    rank_input, rank_feature_gradient = (
        lax.psum(input_part.astype(jnp.bfloat16), ("tensor", "sub")).astype(jnp.float32),
        lax.psum(grad_part.astype(jnp.bfloat16), ("tensor", "sub")).astype(jnp.float32),
    )
    rank_after_dropout = rank_input * dropout_keep
    rank_gradient = adapter_scale * rank_feature_gradient * dropout_keep
    block_count = tenant_count.astype(jnp.float32)[:, None, None]
    block_up_matrix = (
        adapter_scale
        * jnp.einsum(
            "bkr,bkc->brc",
            rank_after_dropout,
            grad_rows.astype(jnp.float32),
            precision=lax.Precision.HIGHEST,
        )
        / block_count
    )
    down_block = (
        jnp.einsum(
            "qjv,qji->qvi",
            rank_gradient,
            input_token_rows.astype(jnp.float32),
            precision=lax.Precision.HIGHEST,
        )
        / block_count
    )
    adapter_term = jnp.einsum(
        "cxm,cmv->cxv",
        rank_gradient,
        block_down_lookup.astype(jnp.float32),
        precision=lax.Precision.HIGHEST,
    ).reshape(tok_rows, width_local)
    partial_terms = jnp.einsum(
        "tc,dc->td", grad_kept, value_matrix, preferred_element_type=jnp.float32
    )
    base = lax.psum_scatter(
        partial_terms.astype(jnp.bfloat16), ("tensor", "sub"), scatter_dimension=1, tiled=True
    ).astype(jnp.float32)
    input_grad = (base + adapter_term).astype(jnp.bfloat16)
    select_full = select.astype(jnp.float32)
    table_down_grad = jnp.einsum(
        "bs,brd->srd", select_full, down_block, precision=lax.Precision.HIGHEST
    )
    table_up_grad = jnp.einsum(
        "bs,brc->src", select_full, block_up_matrix, precision=lax.Precision.HIGHEST
    )
    totals_down, totals_up = (
        lax.psum(table_down_grad.astype(jnp.bfloat16), "dp").astype(jnp.float32),
        lax.psum(table_up_grad.astype(jnp.bfloat16), "dp").astype(jnp.float32),
    )
    first_slot = lax.axis_index("dp") * local_slots
    down_grad = lax.dynamic_slice_in_dim(totals_down, first_slot, local_slots, 0)
    up_grad = lax.dynamic_slice_in_dim(totals_up, first_slot, local_slots, 0)
    return (input_grad, down_grad, up_grad)


def solution(mesh):
    return jax.shard_map(
        body,
        mesh=mesh,
        in_specs=(
            P(("parts", "dp"), ("tensor", "sub")),
            P(("parts", "dp"), ("tensor", "sub")),
            P(None, ("tensor", "sub")),
            P(("parts", "dp"), None, ("tensor", "sub")),
            P(("parts", "dp"), None, ("tensor", "sub")),
            P("parts"),
            P(("parts", "dp")),
            P("parts"),
            P(("parts", "dp")),
        ),
        out_specs=(
            P(("parts", "dp"), ("tensor", "sub")),
            P(("parts", "dp"), None, ("tensor", "sub")),
            P(("parts", "dp"), None, ("tensor", "sub")),
        ),
        check_vma=False,
    )
```

profile of v0, /device:TPU:0, one launch (start us, length us, event | category | flops | bytes accessed | tf_op | source)
XLA Modules:
  0.0 269.9 jit_solution(4983126430828770391)
XLA Ops:
  7.2 0.8 fusion.31
  8.1 0.7 fusion.29
  8.7 1.2 dynamic-slice
  10.9 9.9 %all-reduce = s32[16]{0:T(128)S(1)} all-reduce(s32[16]{0:T(128)S(1)} %dynamic-update-slice), channel_id=2, replica_groups=mesh['parts'=2,'dp'=4,'tensor'=2,'sub'=2] {'dp'}, use_global_device_ids=true, to_apply=%add | all-reduce | flops 16 | bytes 128
  21.2 0.8 select_reduce_fusion.1
  22.0 13.3 %all_gather.14 = bf16[4,16,256]{2,1,0:T(8,128)(2,1)S(1)} all-gather(bf16[1,16,256]{2,1,0:T(8,128)(2,1)} %param.15), channel_id=1, replica_groups=mesh['parts'=2,'dp'=4,'tensor'=2,'sub'=2] {'dp'}, dimensions={0}, use_global_device_ids=true | all-gather | bytes 40960 | tf_op jit(solution)/shard_map/all_gather | solution.py:67
  35.3 14.1 %all_gather.15 = bf16[4,16,2048]{2,1,0:T(8,128)(2,1)S(1)} all-gather(bf16[1,16,2048]{2,1,0:T(8,128)(2,1)} %param.14), channel_id=1, replica_groups=mesh['parts'=2,'dp'=4,'tensor'=2,'sub'=2] {'dp'}, dimensions={0}, use_global_device_ids=true | all-gather | bytes 327680 | tf_op jit(solution)/shard_map/all_gather | solution.py:66
  49.6 0.4 convolution_convert_fusion.1
  50.0 4.0 %fusion.2 = bf16[8,128,16]{1,2,0:T(8,128)(2,1)} fusion(bf16[8,128,2048]{2,1,0:T(8,128)(2,1)} %bitcast.31, bf16[8,16,2048]{2,0,1:T(8,128)(2,1)S(1)} %convolution_convert_fusion.1), kind=kOutput, calls=%fused_computation.14 | convolution fusion | flops 67125248 | bytes 4751360 | tf_op jit(solution)/shard_map/xzu,xtu->xzt/dot_general | solution.py:78
  54.2 0.9 convolution_convert_fusion.6
  55.5 30.2 %all-reduce.7.cloned.1.call-done = (bf16[8,128,16]{1,2,0:T(8,128)(2,1)}, bf16[8,128,16]{1,2,0:T(8,128)(2,1)}) async-done(((bf16[8,128,16]{1,2,0:T(8,128)(2,1)}, bf16[8,128,16]{1,2,0:T(8,128)(2,1)}), (bf16[8,128,16]{1,2,0:T(8,128)(2,1)}, bf16[8,128,16]{1,2,0:T(8,128)(2,1)})) %all-reduce.7.cloned.1.call-update) | async-done | bytes 65552 | tf_op jit(solution)/shard_map/psum | solution.py:86
  85.8 3.5 %convolution_divide_fusion = f32[8,16,2048]{2,1,0:T(8,128)S(1)} fusion(bf16[8,128,2048]{2,1,0:T(8,128)(2,1)} %bitcast.32, f32[8]{0:T(128)S(1)} %get-tuple-element.126, bf16[8,128,16]{1,2,0:T(8,128)(2,1)} %get-tuple-element.124, s32[128,16]{0,1:T(8,128)S(1)} %copy.50, s32[8,128]{1,0:T(8,128)S(1)} %copy.49), kind=kOutput, calls=%fused_computation.5 | convolution fusion | flops 403030016 | bytes 5287968 | tf_op jit(solution)/shard_map/qjv,qji->qvi/dot_general | solution.py:102
  89.3 1.9 convolution_convert_fusion.2
  91.2 10.3 %convolution_convert_fusion = bf16[1024,8192]{1,0:T(8,128)(2,1)} fusion(bf16[1024,256]{1,0:T(8,128)(2,1)S(1)} %broadcast_select_fusion.2, bf16[8192,256]{1,0:T(8,128)(2,1)} %param.13), kind=kOutput, calls=%fused_computation.2 | convolution fusion | flops 4303355904 | bytes 21495808 | tf_op jit(solution)/shard_map/tc,dc->td/dot_general | solution.py:116
  101.6 0.7 copy-done.3
  102.3 0.3 fusion.1
  102.6 0.3 convolution_convert_fusion.4
  102.9 19.2 %psum.31 = bf16[4,16,256]{2,0,1:T(4,128)(2,1)S(1)} all-reduce(bf16[4,16,256]{2,0,1:T(4,128)(2,1)S(1)} %convolution_convert_fusion.4), channel_id=1, replica_groups=mesh['parts'=2,'dp'=4,'tensor'=2,'sub'=2] {'dp'}, use_global_device_ids=true, to_apply=%region_11.12 | all-reduce | flops 16384 | bytes 65536 | tf_op jit(solution)/shard_map/psum | solution.py:132
  122.1 0.6 copy.57
  122.7 5.7 %fusion.5 = f32[8,128,2048]{2,1,0:T(8,128)} fusion(bf16[8,16,2048]{2,0,1:T(8,128)(2,1)S(1)} %convolution_convert_fusion.1, bf16[8,128,16]{1,2,0:T(8,128)(2,1)S(1)} %copy-done.1, s32[128,16]{0,1:T(8,128)S(1)} %copy.50, s32[8,128]{1,0:T(8,128)S(1)} %copy.49), kind=kOutput, calls=%fused_computation.18 | convolution fusion | flops 402767872 | bytes 8957952 | tf_op jit(solution)/shard_map/cxm,cmv->cxv/dot_general | solution.py:110
  128.4 1.1 dynamic-slice_convert_fusion
  129.5 0.7 copy.56
  130.2 124.9 %reduce-scatter.2.cloned.1.call-done = bf16[1024,2048]{1,0:T(8,128)(2,1)} async-done(((bf16[1024,8192]{1,0:T(8,128)(2,1)}), bf16[1024,2048]{1,0:T(8,128)(2,1)}) %reduce-scatter.2.cloned.1.call-update) | async-done | bytes 4194320 | tf_op jit(solution)/shard_map/reduce_scatter | solution.py:119
  255.1 8.3 %fusion = bf16[1024,2048]{1,0:T(8,128)(2,1)} fusion(f32[8,128,2048]{2,1,0:T(8,128)} %fusion.5, bf16[1024,2048]{1,0:T(8,128)(2,1)} %reduce-scatter.2.cloned.1.call-done), kind=kLoop, calls=%fused_computation.4 | loop fusion | flops 6291456 | bytes 16777216 | tf_op jit(solution)/shard_map/convert_element_type | solution.py:122
  (36 shorter events, 1.7 us)
Async XLA Ops:
  7.2 46.9 %copy-start = (bf16[1024,256]{1,0:T(8,128)(2,1)S(1)}, bf16[1024,256]{1,0:T(8,128)(2,1)}, u32[]{:S(2)}) copy-start(bf16[1024,256]{1,0:T(8,128)(2,1)} %param.12) | copy-start | bytes 1572868
  7.2 48.0 %copy-start.2 = (s32[512]{0:T(512)S(1)}, s32[512]{0:T(512)}, u32[]{:S(2)}) copy-start(s32[512]{0:T(512)} %param.19) | copy-start | bytes 6148
  7.2 78.6 %all-reduce.7.cloned.1.call-start = ((), (), s32[]{:S(2)}) async-start(), calls=%async_computation.3 | async-start | bytes 131072 | tf_op jit(solution)/shard_map/psum | solution.py:86
  55.1 73.3 %all-reduce.5.cloned.1.call-start = ((), (), s32[]{:S(2)}) async-start(), calls=%async_computation.2 | async-start | bytes 524288 | tf_op jit(solution)/shard_map/psum | solution.py:131
  91.2 164.0 %reduce-scatter.2.cloned.1.call-start = ((), (), s32[]{:S(2)}) async-start(), calls=%async_computation.1 | async-start | bytes 20971520 | tf_op jit(solution)/shard_map/reduce_scatter | solution.py:119
  101.5 0.8 copy-start.3
  101.5 21.2 %copy-start.1 = (bf16[8,128,16]{1,2,0:T(8,128)(2,1)S(1)}, bf16[8,128,16]{1,2,0:T(8,128)(2,1)}, u32[]{:S(2)}) copy-start(bf16[8,128,16]{1,2,0:T(8,128)(2,1)} %get-tuple-element.124) | copy-start | bytes 98308
Sparse Core Ops, SparseCore 0:
  55.2 30.4 all-reduce.6
  91.3 35.2 all-reduce.4
  129.2 125.8 reduce-scatter.1
where the time goes:
time: 270 us
  waiting for transfers between devices  155 us (57%)
  blocking collectives  56.5 us (21%)
  matrix products  27.4 us (10%)
  between operations  14.5 us (5%)
  other arithmetic  12.2 us (5%)
  local copies, waits for them, and re-layouts  3.93 us (1%)
    reduce_scatter x1, waiting for transfers between devices, body(): lax.psum_scatter(partial_terms.astype(jnp.bfloat16), ('tensor', 'sub'), s...  125 us
    psum x1, waiting for transfers between devices, body(): lax.psum(grad_part.astype(jnp.bfloat16), ('tensor', 'sub'))  30.2 us
    psum x1, blocking collectives, body(): lax.psum(table_up_grad.astype(jnp.bfloat16), 'dp').astype(jnp.float32)  19.2 us
    all_gather x1, blocking collectives, body(): lax.all_gather(adapter_down_table, 'dp', axis=0, tiled=True)  14.1 us
    all_gather x1, blocking collectives, body(): lax.all_gather(adapter_up_table, 'dp', axis=0, tiled=True)  13.3 us
    dot_general x1, matrix products, body(): jnp.einsum('tc,dc->td', grad_kept, value_matrix, preferred_element_type=j...  10.3 us
    unnamed x1, blocking collectives  9.89 us
    convert_element_type x1, other arithmetic, body(): input_grad = (base + adapter_term).astype(jnp.bfloat16)  8.29 us
  transfers between devices with their start and end apart: 3, of which 2 were waited for; matrix products, arithmetic and copies ran while one was open for 7% of the time, Pallas kernels for 0%

commit v1 on v0

v1 whole, which is shorter than its diff:
```python
import functools

import jax
import jax.numpy as jnp
from jax import lax
from jax.experimental import pallas as pl
from jax.experimental.pallas import tpu as pltpu
from jax.sharding import PartitionSpec as P

RANK = 16
BLOCK = 128
SCALE = 2.0
CHUNKS = 2
MESH = pl.DeviceIdType.MESH
F32 = jnp.float32
BF16 = jnp.bfloat16


def dot_nt(a, b):
    return lax.dot_general(a, b, (((1,), (1,)), ((), ())), preferred_element_type=F32)


def exchange(
    sizes,
    x_hbm, dy_ref, w_hbm, down_ref, up_ref, drop_ref, meta_ref, info_ref,
    wfull, dyfull, downall, gexp, live_ref, sums_ref,
    x_ref, downs, ups, infos, part, ranks, outgoing, incoming,
    x_sem, own_sem, tab_send, tab_recv, rk_send, rk_recv, out_send, out_recv,
    wx_send, wx_recv, wz_send, wz_recv, wy_send, wy_recv, wc_send, wc_recv,
    dx_send, dx_recv, dc_send, dc_recv,
):
    n_dp, n_t, n_s = sizes
    a, d, t, s = (lax.axis_index(n) for n in ("parts", "dp", "tensor", "sub"))
    me = t * n_s + s
    rows, width = x_ref.shape
    vl = dy_ref.shape[1]
    rk = down_ref.shape[0]
    quarter = width // 4
    piece = quarter // CHUNKS
    odd = lax.rem(d, 2)
    z_peer = {"dp": d + 1 - 2 * odd}
    y_peer = {"parts": 1 - a}
    core_peer = {"sub": 1 - s}

    def ahead(dt, ds):
        return lax.rem(t + dt, n_t), lax.rem(s + ds, n_s)

    def behind(dt, ds):
        return lax.rem(t - dt + n_t, n_t), lax.rem(s - ds + n_s, n_s)

    group = [(dt, ds) for dt in range(n_t) for ds in range(n_s) if (dt, ds) != (0, 0)]
    cross = [(dt, ds) for dt, ds in group if dt]

    def remote(src, dst, send, recv, peer):
        return pltpu.make_async_remote_copy(
            src_ref=src, dst_ref=dst, send_sem=send, recv_sem=recv,
            device_id=peer, device_id_type=MESH,
        )

    barrier = pltpu.get_barrier_semaphore()
    for dt, ds in group:
        pt, ps = ahead(dt, ds)
        pl.semaphore_signal(barrier, inc=1, device_id={"tensor": pt, "sub": ps}, device_id_type=MESH)
    for off in range(1, n_dp):
        pl.semaphore_signal(barrier, inc=1, device_id={"dp": lax.rem(d + off, n_dp)}, device_id_type=MESH)
    pl.semaphore_signal(barrier, inc=1, device_id=y_peer, device_id_type=MESH)
    x_copy = pltpu.make_async_copy(x_hbm, x_ref, x_sem)
    x_copy.start()
    downs[d] = down_ref[...]
    ups[d] = up_ref[...]
    pl.semaphore_wait(barrier, len(group) + n_dp)

    sent = []

    def go(copy):
        copy.start()
        sent.append(copy)

    for off in range(1, n_dp):
        to = {"dp": lax.rem(d + off, n_dp)}
        go(remote(info_ref, infos.at[off], tab_send.at[0, off], tab_recv.at[0, off], to))
        go(remote(up_ref, ups.at[d], tab_send.at[1, off], tab_recv.at[1, off], to))
        go(remote(down_ref, downs.at[d], tab_send.at[2, off], tab_recv.at[2, off], to))

    def span(q, c):
        return pl.ds(pl.multiple_of(q * quarter + c * piece, 16), piece)

    q_own = 2 * a + odd
    q_z = 2 * a + 1 - odd
    q_y = 2 * (1 - a) + odd
    q_yz = 2 * (1 - a) + 1 - odd
    for c in range(CHUNKS):
        for dt, ds in cross:
            pt, ps = ahead(dt, ds)
            start = (pt * n_s + ps) * width + q_own * quarter + c * piece
            src = w_hbm.at[pl.ds(pl.multiple_of(start, 16), piece)]
            k = dt * n_s + ds
            go(remote(src, wfull.at[me, span(q_own, c)], wx_send.at[k, c], wx_recv.at[k, c],
                      {"tensor": pt, "sub": ps}))

    for dt in range(1, n_t):
        go(remote(dy_ref, dyfull.at[me], dx_send.at[dt], dx_recv.at[dt], {"tensor": lax.rem(t + dt, n_t)}))
    go(remote(dy_ref, dyfull.at[me], dc_send.at[0], dc_recv.at[0], core_peer))
    other_rows = pl.ds(pl.multiple_of((t * n_s + 1 - s) * width, 16), width)
    go(remote(w_hbm.at[other_rows], wfull.at[me], wc_send, wc_recv, core_peer))
    own_w = pltpu.make_async_copy(
        w_hbm.at[pl.ds(pl.multiple_of(me * width, 16), width)], wfull.at[me], own_sem.at[0])
    own_w.start()
    own_dy = pltpu.make_async_copy(dy_ref, dyfull.at[me], own_sem.at[1])
    own_dy.start()

    for off in range(1, n_dp):
        frm = lax.rem(d - off + n_dp, n_dp)
        here = {"dp": frm}
        remote(info_ref, infos.at[off], tab_send.at[0, off], tab_recv.at[0, off], here).wait_recv()
        remote(up_ref, ups.at[frm], tab_send.at[1, off], tab_recv.at[1, off], here).wait_recv()
        remote(down_ref, downs.at[frm], tab_send.at[2, off], tab_recv.at[2, off], here).wait_recv()
    x_copy.wait()
    slots = n_dp * rk // RANK
    slot_tok = meta_ref[0:1, :]
    own_slot = lax.broadcasted_iota(jnp.int32, (slots, RANK, rows), 0) == slot_tok[None]
    down_map = downs[...].reshape(n_dp * rk, width)
    up_map = ups[...].reshape(n_dp * rk, vl)
    downall[...] = down_map
    in_all = dot_nt(down_map, x_ref[...]).reshape(slots, RANK, rows)
    grad_all = dot_nt(up_map, dy_ref[...]).reshape(slots, RANK, rows)
    part[0:RANK, :] = jnp.sum(jnp.where(own_slot, in_all, 0.0), 0).astype(BF16)
    part[RANK:2 * RANK, :] = jnp.sum(jnp.where(own_slot, grad_all, 0.0), 0).astype(BF16)
    for dt, ds in group:
        pt, ps = ahead(dt, ds)
        k = dt * n_s + ds
        go(remote(part, ranks.at[me], rk_send.at[k], rk_recv.at[k], {"tensor": pt, "sub": ps}))
    ranks[me] = part[...]

    def forward(dt, ds, c):
        ft, fs = behind(dt, ds)
        g = ft * n_s + fs
        k = dt * n_s + ds
        mine = wfull.at[g, span(q_own, c)]
        remote(mine, mine, wx_send.at[k, c], wx_recv.at[k, c], {"tensor": ft, "sub": fs}).wait_recv()
        go(remote(mine, mine, wz_send.at[k, c], wz_recv.at[k, c], z_peer))
        go(remote(mine, mine, wy_send.at[0, k, c], wy_recv.at[0, k, c], y_peer))

    for c in range(CHUNKS):
        for dt, ds in cross:
            forward(dt, ds, c)

    lane = lax.broadcasted_iota(jnp.int32, (1, rows), 1)
    limit = meta_ref[1:2, :]
    tenant = meta_ref[2:3, :]
    following = jnp.concatenate([infos[n_dp - 1, 0:1, :]] * (rows // BLOCK), axis=1)
    last_block = lane >= rows - BLOCK
    goes_on = last_block & (following == tenant) & (jnp.zeros_like(lane) + d < n_dp - 1)
    limit = jnp.where(goes_on, BLOCK, limit)
    live = (lax.rem(lane, BLOCK) < limit).astype(F32)
    live_ref[...] = jnp.broadcast_to(live, live_ref.shape)

    for dt, ds in group:
        ft, fs = behind(dt, ds)
        k = dt * n_s + ds
        remote(part, ranks.at[ft * n_s + fs], rk_send.at[k], rk_recv.at[k],
               {"tensor": ft, "sub": fs}).wait_recv()
    total = jnp.sum(ranks[...].astype(F32), 0)
    keep = drop_ref[...] * (SCALE * live)
    dropped = total[0:RANK] * keep
    grad_rank = total[RANK:2 * RANK] * keep
    dropped_all = jnp.where(own_slot, dropped[None], 0.0).reshape(n_dp * rk, rows).astype(BF16)
    grad_all = jnp.where(own_slot, grad_rank[None], 0.0).reshape(n_dp * rk, rows).astype(BF16)
    gexp[...] = grad_all
    up_part = jnp.dot(dropped_all, dy_ref[...], preferred_element_type=F32)
    outgoing[:, :, width:] = up_part.reshape(n_dp, rk, vl).astype(BF16)
    down_part = jnp.dot(grad_all, x_ref[...], preferred_element_type=F32)
    outgoing[:, :, :width] = down_part.reshape(n_dp, rk, width).astype(BF16)
    for off in range(1, n_dp):
        to = lax.rem(d + off, n_dp)
        go(remote(outgoing.at[to], incoming.at[off], out_send.at[off], out_recv.at[off], {"dp": to}))
    incoming[0] = outgoing[d]

    for c in range(CHUNKS):
        for dt, ds in cross:
            ft, fs = behind(dt, ds)
            k = dt * n_s + ds
            got = wfull.at[ft * n_s + fs, span(q_z, c)]
            remote(got, got, wz_send.at[k, c], wz_recv.at[k, c], z_peer).wait_recv()
            go(remote(got, got, wy_send.at[1, k, c], wy_recv.at[1, k, c], y_peer))
    for dt in range(1, n_t):
        ft = lax.rem(t - dt + n_t, n_t)
        got = dyfull.at[ft * n_s + s]
        remote(got, got, dx_send.at[dt], dx_recv.at[dt], {"tensor": ft}).wait_recv()
        go(remote(got, got, dc_send.at[dt], dc_recv.at[dt], core_peer))

    for off in range(1, n_dp):
        remote(outgoing.at[d], incoming.at[off], out_send.at[off], out_recv.at[off],
               {"dp": lax.rem(d - off + n_dp, n_dp)}).wait_recv()
    sums_ref[...] = jnp.sum(incoming[...].astype(F32), 0)

    for c in range(CHUNKS):
        for dt, ds in cross:
            ft, fs = behind(dt, ds)
            g = ft * n_s + fs
            k = dt * n_s + ds
            for j, q in enumerate((q_y, q_yz)):
                got = wfull.at[g, span(q, c)]
                remote(got, got, wy_send.at[j, k, c], wy_recv.at[j, k, c], y_peer).wait_recv()
    for dt in range(n_t):
        got = dyfull.at[lax.rem(t - dt + n_t, n_t) * n_s + 1 - s]
        remote(got, got, dc_send.at[dt], dc_recv.at[dt], core_peer).wait_recv()
    got = wfull.at[t * n_s + 1 - s]
    remote(got, got, wc_send, wc_recv, core_peer).wait_recv()
    own_w.wait()
    own_dy.wait()
    for copy in sent:
        copy.wait_send()


def product(dy_ref, w_ref, down_ref, gexp_ref, live_ref, out_ref, kept, ranked):
    groups, rows, _ = dy_ref.shape

    @pl.when(pl.program_id(0) == 0)
    def _():
        eye = lax.broadcasted_iota(jnp.int32, (BLOCK, BLOCK), 0) == lax.broadcasted_iota(
            jnp.int32, (BLOCK, BLOCK), 1)
        for b in range(rows // BLOCK):
            at = slice(b * BLOCK, (b + 1) * BLOCK)
            column = jnp.sum(jnp.where(eye, live_ref[0:1, at], 0.0), 1, keepdims=True)
            for g in range(groups):
                kept[g, at, :] = jnp.where(column > 0, dy_ref[g, at, :].astype(F32), 0.0).astype(BF16)
        ranked[...] = gexp_ref[...].astype(F32).T.astype(BF16)

    total = jnp.dot(ranked[...], down_ref[...], preferred_element_type=F32)
    for g in range(groups):
        total += dot_nt(kept[g], w_ref[g])
    out_ref[...] = total.astype(BF16)


def body(x, dy, w, down_table, up_table, live_token_count, block_customer, customer_slot, dropout_flags):
    n_dp, n_t, n_s = (lax.axis_size(n) for n in ("dp", "tensor", "sub"))
    groups = n_t * n_s
    tenants = live_token_count.shape[0]
    blocks = block_customer.shape[0]
    rows, width = x.shape
    vl = dy.shape[1]
    local_slots = down_table.shape[0]
    rk = local_slots * RANK
    onehot = (block_customer[:, None] == jnp.arange(tenants, dtype=jnp.int32)[None, :]).astype(jnp.int32)
    count = jnp.sum(onehot * live_token_count[None, :], 1)
    slot = jnp.sum(onehot * customer_slot[None, :], 1)
    tail = count - BLOCK * ((count + BLOCK - 1) // BLOCK - 1)
    ends = jnp.concatenate([block_customer[1:] != block_customer[:-1], jnp.ones((1,), bool)])
    limit = jnp.where(ends, tail, BLOCK)
    meta = jnp.stack([slot, limit, block_customer] + [slot] * 5)
    meta = jnp.broadcast_to(meta[:, :, None], (8, blocks, BLOCK)).reshape(8, rows)
    info = jnp.broadcast_to(block_customer[0], (8, BLOCK))
    shifts = jnp.arange(RANK, dtype=jnp.int32)[:, None, None] + 16 * jnp.arange(2, dtype=jnp.int32)[None, None, :]
    bits = jnp.bitwise_and(jnp.right_shift(dropout_flags[None, :, None], shifts), 1)
    drop = (2.0 * bits.astype(F32)).reshape(RANK, rows)

    vmem = pl.BlockSpec(memory_space=pltpu.VMEM)
    hbm = pl.BlockSpec(memory_space=pl.ANY)
    dma = pltpu.SemaphoreType.DMA
    all_rk = n_dp * rk
    wfull, dyfull, downall, gexp, live, sums = pl.pallas_call(
        functools.partial(exchange, (n_dp, n_t, n_s)),
        out_shape=(
            jax.ShapeDtypeStruct((groups, width, vl), BF16),
            jax.ShapeDtypeStruct((groups, rows, vl), BF16),
            jax.ShapeDtypeStruct((all_rk, width), BF16),
            jax.ShapeDtypeStruct((all_rk, rows), BF16),
            jax.ShapeDtypeStruct((8, rows), F32),
            jax.ShapeDtypeStruct((rk, width + vl), F32),
        ),
        in_specs=[hbm, vmem, hbm] + [vmem] * 5,
        out_specs=(hbm, hbm, vmem, vmem, vmem, vmem),
        scratch_shapes=[
            pltpu.VMEM((rows, width), BF16),
            pltpu.VMEM((n_dp, rk, width), BF16),
            pltpu.VMEM((n_dp, rk, vl), BF16),
            pltpu.VMEM((n_dp, 8, BLOCK), jnp.int32),
            pltpu.VMEM((2 * RANK, rows), BF16),
            pltpu.VMEM((groups, 2 * RANK, rows), BF16),
            pltpu.VMEM((n_dp, rk, width + vl), BF16),
            pltpu.VMEM((n_dp, rk, width + vl), BF16),
            dma, dma((2,)),
            dma((3, n_dp)), dma((3, n_dp)),
            dma((groups,)), dma((groups,)),
            dma((n_dp,)), dma((n_dp,)),
            dma((groups, CHUNKS)), dma((groups, CHUNKS)),
            dma((groups, CHUNKS)), dma((groups, CHUNKS)),
            dma((2, groups, CHUNKS)), dma((2, groups, CHUNKS)),
            dma, dma,
            dma((n_t,)), dma((n_t,)),
            dma((n_t,)), dma((n_t,)),
        ],
        compiler_params=pltpu.CompilerParams(
            collective_id=0, has_side_effects=True, vmem_limit_bytes=40 * 1024 * 1024
        ),
    )(x, dy, w, down_table.reshape(rk, width), up_table.reshape(rk, vl), drop, meta, info)

    tile = 256
    input_grad = pl.pallas_call(
        product,
        grid=(width // tile,),
        out_shape=jax.ShapeDtypeStruct((rows, width), BF16),
        in_specs=[
            pl.BlockSpec((groups, rows, vl), lambda j: (0, 0, 0)),
            pl.BlockSpec((groups, tile, vl), lambda j: (0, j, 0)),
            pl.BlockSpec((all_rk, tile), lambda j: (0, j)),
            pl.BlockSpec((all_rk, rows), lambda j: (0, 0)),
            pl.BlockSpec((8, rows), lambda j: (0, 0)),
        ],
        out_specs=pl.BlockSpec((rows, tile), lambda j: (0, j)),
        scratch_shapes=[pltpu.VMEM((groups, rows, vl), BF16), pltpu.VMEM((rows, all_rk), BF16)],
        compiler_params=pltpu.CompilerParams(vmem_limit_bytes=40 * 1024 * 1024),
    )(dyfull, wfull, downall, gexp, live)

    mine = lax.axis_index("dp") * local_slots + jnp.arange(local_slots, dtype=jnp.int32)
    chosen = (customer_slot[None, :] == mine[:, None]).astype(jnp.int32)
    slot_count = jnp.sum(chosen * live_token_count[None, :], 1).astype(F32)[:, None, None]
    sums = sums.reshape(local_slots, RANK, width + vl)
    return input_grad, sums[:, :, :width] / slot_count, sums[:, :, width:] / slot_count


def solution(mesh):
    return jax.shard_map(
        body,
        mesh=mesh,
        in_specs=(
            P(("parts", "dp"), ("tensor", "sub")),
            P(("parts", "dp"), ("tensor", "sub")),
            P(None, ("tensor", "sub")),
            P(("parts", "dp"), None, ("tensor", "sub")),
            P(("parts", "dp"), None, ("tensor", "sub")),
            P("parts"),
            P(("parts", "dp")),
            P("parts"),
            P(("parts", "dp")),
        ),
        out_specs=(
            P(("parts", "dp"), ("tensor", "sub")),
            P(("parts", "dp"), None, ("tensor", "sub")),
            P(("parts", "dp"), None, ("tensor", "sub")),
        ),
        check_vma=False,
    )
```

time: 270 us -> 69.2 us (0.26)
  waiting for transfers between devices: 155 us -> 0 us
  blocking collectives: 56.5 us -> 0 us
  Pallas kernels: 0 us -> 56.3 us
  matrix products: 27.4 us -> 0 us
  between operations: 14.5 us -> 1.36 us
  other arithmetic: 12.2 us -> 3.67 us
  local copies, waits for them, and re-layouts: 3.93 us -> 7.53 us
    reduce_scatter x1 -> x0, waiting for transfers between devices: 125 us -> none  [body(): lax.psum_scatter(partial_terms.astype(jnp.bfloat16), ('tensor', 'sub'), s...]
    pallas_call x0 -> x2, Pallas kernels: none -> 56.3 us  [the longest x1 47.8 us: body(): pl.pallas_call(functools.partial(exchange, (n_dp, n_t, n_s)), out_shape=(...]
    psum x2 -> x0, waiting for transfers between devices: 30.2 us -> none  [the longest x1 30.2 us: body(): lax.psum(grad_part.astype(jnp.bfloat16), ('tensor', 'sub'))]
    dot_general x10 -> x0, matrix products: 27.4 us -> none  [the longest x1 10.3 us: body(): jnp.einsum('tc,dc->td', grad_kept, value_matrix, preferred_element_type=j...]
    all_gather x2 -> x0, blocking collectives: 27.4 us -> none  [the longest x1 14.1 us: body(): lax.all_gather(adapter_down_table, 'dp', axis=0, tiled=True)]
    psum x1 -> x0, blocking collectives: 19.2 us -> none  [body(): lax.psum(table_up_grad.astype(jnp.bfloat16), 'dp').astype(jnp.float32)]
    convert_element_type x5 -> x0, other arithmetic: 10 us -> none  [the longest x1 8.29 us: body(): input_grad = (base + adapter_term).astype(jnp.bfloat16)]
    unnamed x1 -> x0, blocking collectives: 9.89 us -> none
  transfers between devices with their start and end apart: 3 -> 0, of which waited for: 2 -> 0; matrix products, arithmetic and copies ran while one was open for 7% -> 0% of each run, Pallas kernels for 0% -> 0%
where the time goes in v1:
time: 69.2 us; the launch traced here: 68.9 us
  Pallas kernels  56.3 us (81%)
  local copies, waits for them, and re-layouts  7.53 us (11%)
  other arithmetic  3.67 us (5%)
  between operations  1.36 us (2%)
    pallas_call x1, Pallas kernels, body(): pl.pallas_call(functools.partial(exchange, (n_dp, n_t, n_s)), out_shape=(...  47.8 us
    pallas_call x1, Pallas kernels, body(): pl.pallas_call(product, grid=(width // tile,), out_shape=jax.ShapeDtypeSt...  8.51 us
    unnamed x12, local copies, waits for them, and re-layouts  4.77 us

profile of v1, /device:TPU:0, one launch (start us, length us, event | category | flops | bytes accessed | tf_op | source)
XLA Modules:
  0.0 68.9 jit_solution(16136715171035736023)
XLA Ops:
  0.6 0.8 %select_reduce_fusion = (s32[8]{0:T(128)S(1)}, s32[8]{0:T(128)S(1)}) fusion(s32[4]{0:T(128)} %param.14, s32[8]{0:T(128)} %param.15, s32[4]{0:T(128)} %param.16), kind=kLoop, calls=%fused_computation.4 | loop fusion | flops 144 | bytes 128 | tf_op jit(solution)/shard_map/reduce_sum | solution.py:246
  1.4 0.8 %compare_bitcast_fusion = pred[1,7]{1,0:T(4,128)(4,1)S(1)} fusion(s32[8]{0:T(128)} %param.15), kind=kLoop, calls=%fused_computation.10 | loop fusion | flops 7 | bytes 63 | tf_op jit(solution)/shard_map/concatenate | solution.py:249
  2.2 0.1 add_select_fusion
  2.3 0.7 stack.8
  3.0 0.1 copy.16
  3.0 0.1 broadcast_bitcast_fusion.meta_ref
  3.1 0.1 iota_add_fusion
  3.2 0.1 shift_right_arithmetic.23
  3.3 0.2 copy.15
  3.5 0.8 %shift_right_arithmetic.20 = s32[512,2]{1,0:T(8,128)S(1)} broadcast(s32[512]{0:T(512)} %param.17), dimensions={0} | broadcast | bytes 6144 | tf_op jit(solution)/shard_map/shift_right_arithmetic | solution.py:255
  4.3 0.2 shift_right_arithmetic.21
  4.5 0.6 broadcast_in_dim.7.info_ref
  5.2 0.0 copy-start
  5.2 2.2 %copy-done = bf16[1024,2048]{1,0:T(8,128)(2,1)S(1)} copy-done((bf16[1024,2048]{1,0:T(8,128)(2,1)S(1)}, bf16[1024,2048]{1,0:T(8,128)(2,1)}, u32[]{:S(2)}) %copy-start) | copy-done | bytes 4194328
  7.4 1.0 %copy-done.1 = bf16[1024,256]{1,0:T(8,128)(2,1)S(1)} copy-done((bf16[1024,256]{1,0:T(8,128)(2,1)S(1)}, bf16[1024,256]{1,0:T(8,128)(2,1)}, u32[]{:S(2)}) %copy-start.1) | copy-done | bytes 524312
  8.4 0.8 %copy-done.2 = bf16[1,16,2048]{2,1,0:T(8,128)(2,1)S(1)} copy-done((bf16[1,16,2048]{2,1,0:T(8,128)(2,1)S(1)}, bf16[1,16,2048]{2,1,0:T(8,128)(2,1)}, u32[]{:S(2)}) %copy-start.2) | copy-done | bytes 65560
  9.2 0.7 %copy-done.3 = bf16[1,16,256]{2,1,0:T(8,128)(2,1)S(1)} copy-done((bf16[1,16,256]{2,1,0:T(8,128)(2,1)S(1)}, bf16[1,16,256]{2,1,0:T(8,128)(2,1)}, u32[]{:S(2)}) %copy-start.3) | copy-done | bytes 8216
  9.9 47.8 %shard_map.112 = (bf16[4,2048,256]{2,1,0:T(8,128)(2,1)S(1)}, bf16[4,1024,256]{2,1,0:T(8,128)(2,1)S(1)}, bf16[64,2048]{1,0:T(8,128)(2,1)S(1)}, bf16[64,1024]{1,0:...) custom-call(bf16[1024,2048]{1,0:T(8,128)(2,1)S(1)} %copy-done, bf16[1024,256]{1,0:T(8,128)(2,1)S(1)} %copy-done.1, ...), custom_call_target="tpu_custom_call" | custom-call | tf_op jit(solution)/shard_map/pallas_call | solution.py:262
  57.8 0.0 copy-start.4
  57.8 0.0 copy-start.5
  57.8 8.5 %shard_map.113 = bf16[1024,2048]{1,0:T(8,128)(2,1)} custom-call(bf16[4,1024,256]{2,1,0:T(8,128)(2,1)S(1)} %get-tuple-element.9.dy_ref, bf16[4,2048,256]{2,1,0:T(8,128)(2,1)S(1)} %get-tuple-element.10.w_ref, bf16[64,2048]{1,0:T(8,128)(2,1)S(1)} %get-tuple-element.11.down_ref, bf16[64,1024]{1,0:T(8,128)(2,1)S(1)} %get-tuple-element.12.gexp_ref, ...), custom_call_target="tpu_custom_call" | custom-call | tf_op jit(solution)/shard_map/pallas_call | solution.py:300
  66.3 0.6 fusion
  67.6 0.7 slice_divide_fusion
  68.3 0.6 slice_divide_fusion.1
  (7 shorter events, 0.0 us)
Async XLA Ops:
  5.2 2.2 %copy-start = (bf16[1024,2048]{1,0:T(8,128)(2,1)S(1)}, bf16[1024,2048]{1,0:T(8,128)(2,1)}, u32[]{:S(2)}) copy-start(bf16[1024,2048]{1,0:T(8,128)(2,1)} %x_hbm.1) | copy-start | bytes 12582916
  7.4 1.0 %copy-start.1 = (bf16[1024,256]{1,0:T(8,128)(2,1)S(1)}, bf16[1024,256]{1,0:T(8,128)(2,1)}, u32[]{:S(2)}) copy-start(bf16[1024,256]{1,0:T(8,128)(2,1)} %dy_ref.1) | copy-start | bytes 1572868
  8.4 0.8 %copy-start.2 = (bf16[1,16,2048]{2,1,0:T(8,128)(2,1)S(1)}, bf16[1,16,2048]{2,1,0:T(8,128)(2,1)}, u32[]{:S(2)}) copy-start(bf16[1,16,2048]{2,1,0:T(8,128)(2,1)} %param.12) | copy-start | bytes 196612
  9.2 0.7 %copy-start.3 = (bf16[1,16,256]{2,1,0:T(8,128)(2,1)S(1)}, bf16[1,16,256]{2,1,0:T(8,128)(2,1)}, u32[]{:S(2)}) copy-start(bf16[1,16,256]{2,1,0:T(8,128)(2,1)} %param.13) | copy-start | bytes 24580
  57.8 8.5 %copy-start.4 = (s32[4]{0:T(128)S(1)}, s32[4]{0:T(128)}, u32[]{:S(2)}) copy-start(s32[4]{0:T(128)} %param.14) | copy-start | bytes 52
  57.8 8.5 %copy-start.5 = (s32[4]{0:T(128)S(1)}, s32[4]{0:T(128)}, u32[]{:S(2)}) copy-start(s32[4]{0:T(128)} %param.16) | copy-start | bytes 52

commit v2 on v1

v2 whole, which is shorter than its diff:
```python
import functools

import jax
import jax.numpy as jnp
from jax import lax
from jax.experimental import pallas as pl
from jax.experimental.pallas import tpu as pltpu
from jax.sharding import PartitionSpec as P

RANK = 16
BLOCK = 128
SCALE = 2.0
TILE = 256
MESH = pl.DeviceIdType.MESH
F32 = jnp.float32
BF16 = jnp.bfloat16


def dot_nt(a, b):
    return lax.dot_general(a, b, (((1,), (1,)), ((), ())), preferred_element_type=F32)


def dot_nn(a, b):
    return jnp.dot(a, b, preferred_element_type=F32)


def kernel(
    sizes,
    x_hbm, dy_hbm, w_hbm, down_hbm, up_hbm, live_count, customer, slot_of, flags_ref,
    out_ref, down_out, up_out,
    x_ref, wfull, dyfull, acc, downs, ups, info, infos, part, ranks, outgoing, incoming, keep_rows, ranked,
    own_sem, tab_send, tab_recv, rk_send, rk_recv, out_send, out_recv,
    wx_send, wx_recv, wz_send, wz_recv, wy_send, wy_recv, wd_send, wd_recv, wc_send, wc_recv,
    dx_send, dx_recv, dc_send, dc_recv,
):
    n_dp, n_t, n_s = sizes
    a, d, t, s = (lax.axis_index(n) for n in ("parts", "dp", "tensor", "sub"))
    me = t * n_s + s
    rows, width = x_ref.shape
    vl = dyfull.shape[2]
    rk = down_hbm.shape[0]
    local_slots = rk // RANK
    blocks = rows // BLOCK
    tenants = live_count.shape[0]
    quarter = width // 4
    piece = quarter // 2
    half = rows // 2
    odd = lax.rem(d, 2)
    z_peer = {"dp": d + 1 - 2 * odd}
    y_peer = {"parts": 1 - a}
    core_peer = {"sub": 1 - s}

    def ahead(dt, ds):
        return lax.rem(t + dt, n_t), lax.rem(s + ds, n_s)

    def behind(dt, ds):
        return lax.rem(t - dt + n_t, n_t), lax.rem(s - ds + n_s, n_s)

    group = [(dt, ds) for dt in range(n_t) for ds in range(n_s) if (dt, ds) != (0, 0)]
    cross = [(dt, ds) for dt, ds in group if dt]

    def remote(src, dst, send, recv, peer):
        return pltpu.make_async_remote_copy(
            src_ref=src, dst_ref=dst, send_sem=send, recv_sem=recv,
            device_id=peer, device_id_type=MESH,
        )

    barrier = pltpu.get_barrier_semaphore()
    for dt, ds in group:
        pt, ps = ahead(dt, ds)
        pl.semaphore_signal(barrier, inc=1, device_id={"tensor": pt, "sub": ps}, device_id_type=MESH)
    for off in range(1, n_dp):
        pl.semaphore_signal(barrier, inc=1, device_id={"dp": lax.rem(d + off, n_dp)}, device_id_type=MESH)
    pl.semaphore_signal(barrier, inc=1, device_id=y_peer, device_id_type=MESH)

    own_rows = pl.ds(pl.multiple_of(me * width, 16), width)
    own = [
        pltpu.make_async_copy(down_hbm, downs.at[d], own_sem.at[0]),
        pltpu.make_async_copy(up_hbm, ups.at[d], own_sem.at[1]),
        pltpu.make_async_copy(dy_hbm, dyfull.at[me], own_sem.at[2]),
        pltpu.make_async_copy(x_hbm, x_ref, own_sem.at[3]),
        pltpu.make_async_copy(w_hbm.at[own_rows], wfull.at[me], own_sem.at[4]),
    ]
    for copy in own:
        copy.start()
    info[...] = jnp.full(info.shape, customer[0], jnp.int32)

    word = flags_ref[...]
    rank_row = lax.broadcasted_iota(jnp.int32, (RANK, word.shape[1]), 0)
    word = jnp.broadcast_to(word, rank_row.shape)
    spread_row = lax.broadcasted_iota(jnp.int32, (BLOCK, 2 * BLOCK), 0)
    spread_lane = lax.broadcasted_iota(jnp.int32, (BLOCK, 2 * BLOCK), 1)
    drops = []
    for h in range(2):
        bits = jnp.bitwise_and(jnp.right_shift(word, rank_row + RANK * h), 1).astype(F32).astype(BF16)
        spread = (spread_lane == 2 * spread_row + h).astype(F32).astype(BF16)
        drops.append(jnp.concatenate(
            [dot_nn(bits[:, j * BLOCK:(j + 1) * BLOCK], spread) for j in range(rows // (2 * BLOCK))], axis=1))
    drop = 2.0 * (drops[0] + drops[1])

    slot_parts, limits = [], []
    for b in range(blocks):
        who = customer[b]
        count = live_count[who]
        tail = count - BLOCK * (jnp.right_shift(count + (BLOCK - 1), 7) - 1)
        if b + 1 < blocks:
            tail = jnp.where(customer[b + 1] == who, BLOCK, tail)
        slot_parts.append(jnp.full((1, BLOCK), slot_of[who], jnp.int32))
        limits.append(jnp.full((1, BLOCK), tail, jnp.int32))
    slot_tok = jnp.concatenate(slot_parts, axis=1)

    pl.semaphore_wait(barrier, len(group) + n_dp)
    sent = []

    def go(copy):
        copy.start()
        sent.append(copy)

    for off in range(1, n_dp):
        to = {"dp": lax.rem(d + off, n_dp)}
        go(remote(info, infos.at[off], tab_send.at[0, off], tab_recv.at[0, off], to))
        go(remote(up_hbm, ups.at[d], tab_send.at[1, off], tab_recv.at[1, off], to))
        go(remote(down_hbm, downs.at[d], tab_send.at[2, off], tab_recv.at[2, off], to))

    def span(q, c):
        return pl.ds(pl.multiple_of(q * quarter + c * piece, 16), piece)

    q_own = 2 * a + odd
    q_z = 2 * a + 1 - odd
    q_y = 2 * (1 - a) + odd
    q_yz = 2 * (1 - a) + 1 - odd
    for c in range(2):
        for dt, ds in cross:
            pt, ps = ahead(dt, ds)
            start = (pt * n_s + ps) * width + q_own * quarter + c * piece
            src = w_hbm.at[pl.ds(pl.multiple_of(start, 16), piece)]
            k = dt * n_s + ds
            go(remote(src, wfull.at[me, span(q_own, c)], wx_send.at[k, c], wx_recv.at[k, c],
                      {"tensor": pt, "sub": ps}))

    def send_dy(c):
        at = pl.ds(c * half, half)
        for dt in range(1, n_t):
            go(remote(dy_hbm.at[at], dyfull.at[me, at], dx_send.at[dt, c], dx_recv.at[dt, c],
                      {"tensor": lax.rem(t + dt, n_t)}))

    send_dy(0)
    go(remote(dy_hbm, dyfull.at[me], dc_send.at[0, 0], dc_recv.at[0, 0], core_peer))
    other_rows = pl.ds(pl.multiple_of((t * n_s + 1 - s) * width, 16), width)
    go(remote(w_hbm.at[other_rows], wfull.at[me], wc_send, wc_recv, core_peer))

    def forward(c):
        for dt, ds in cross:
            ft, fs = behind(dt, ds)
            k = dt * n_s + ds
            got = wfull.at[ft * n_s + fs, span(q_own, c)]
            remote(got, got, wx_send.at[k, c], wx_recv.at[k, c], {"tensor": ft, "sub": fs}).wait_recv()
            go(remote(got, got, wz_send.at[k, c], wz_recv.at[k, c], z_peer))
            go(remote(got, got, wy_send.at[k, c], wy_recv.at[k, c], y_peer))

    for copy in own:
        copy.wait()
    for off in range(1, n_dp):
        frm = lax.rem(d - off + n_dp, n_dp)
        here = {"dp": frm}
        remote(info, infos.at[off], tab_send.at[0, off], tab_recv.at[0, off], here).wait_recv()
        remote(up_hbm, ups.at[frm], tab_send.at[1, off], tab_recv.at[1, off], here).wait_recv()
        remote(down_hbm, downs.at[frm], tab_send.at[2, off], tab_recv.at[2, off], here).wait_recv()
    forward(0)
    slots = n_dp * local_slots
    own_slot = lax.broadcasted_iota(jnp.int32, (slots, RANK, rows), 0) == slot_tok[None]
    in_all = dot_nt(downs[...].reshape(n_dp * rk, width), x_ref[...]).reshape(slots, RANK, rows)
    grad_all = dot_nt(ups[...].reshape(n_dp * rk, vl), dyfull[me]).reshape(slots, RANK, rows)
    part[0:RANK, :] = jnp.sum(jnp.where(own_slot, in_all, 0.0), 0).astype(BF16)
    part[RANK:2 * RANK, :] = jnp.sum(jnp.where(own_slot, grad_all, 0.0), 0).astype(BF16)
    for dt, ds in group:
        pt, ps = ahead(dt, ds)
        k = dt * n_s + ds
        go(remote(part, ranks.at[me], rk_send.at[k], rk_recv.at[k], {"tensor": pt, "sub": ps}))
    send_dy(1)
    ranks[me] = part[...]

    following = infos[n_dp - 1, 0:1, :]
    goes_on = (following == customer[blocks - 1]) & (jnp.zeros_like(following) + d < n_dp - 1)
    limits[-1] = jnp.where(goes_on, BLOCK, limits[-1])
    limit = jnp.concatenate(limits, axis=1)
    lane = lax.broadcasted_iota(jnp.int32, (1, rows), 1)
    live = (jnp.bitwise_and(lane, BLOCK - 1) < limit).astype(F32)
    eye = lax.broadcasted_iota(jnp.int32, (BLOCK, BLOCK), 0) == lax.broadcasted_iota(
        jnp.int32, (BLOCK, BLOCK), 1)
    for b in range(blocks):
        at = slice(b * BLOCK, (b + 1) * BLOCK)
        column = jnp.sum(jnp.where(eye, live[:, at], 0.0), 1, keepdims=True)
        keep_rows[at, :] = jnp.broadcast_to(column, (BLOCK, BLOCK))
    forward(1)

    got = dyfull.at[t * n_s + 1 - s]
    remote(got, got, dc_send.at[0, 0], dc_recv.at[0, 0], core_peer).wait_recv()
    got = wfull.at[t * n_s + 1 - s]
    remote(got, got, wc_send, wc_recv, core_peer).wait_recv()

    @pl.loop(0, width // TILE)
    def _(j):
        at = pl.ds(pl.multiple_of(j * TILE, TILE), TILE)
        total = dot_nt(dyfull[t * n_s], wfull[t * n_s, at])
        for i in range(1, n_s):
            total += dot_nt(dyfull[t * n_s + i], wfull[t * n_s + i, at])
        acc[:, at] = total

    for dt, ds in group:
        ft, fs = behind(dt, ds)
        k = dt * n_s + ds
        remote(part, ranks.at[ft * n_s + fs], rk_send.at[k], rk_recv.at[k],
               {"tensor": ft, "sub": fs}).wait_recv()
    total = jnp.sum(ranks[...].astype(F32), 0)
    keep = drop * (SCALE * live)
    dropped = total[0:RANK] * keep
    grad_rank = total[RANK:2 * RANK] * keep
    dropped_all = jnp.where(own_slot, dropped[None], 0.0).reshape(n_dp * rk, rows).astype(BF16)
    grad_all = jnp.where(own_slot, grad_rank[None], 0.0).reshape(n_dp * rk, rows)
    up_part = dot_nn(dropped_all, dyfull[me])
    outgoing[:, :, width:] = up_part.reshape(n_dp, rk, vl).astype(BF16)
    down_part = dot_nn(grad_all.astype(BF16), x_ref[...])
    outgoing[:, :, :width] = down_part.reshape(n_dp, rk, width).astype(BF16)
    for off in range(1, n_dp):
        to = lax.rem(d + off, n_dp)
        go(remote(outgoing.at[to], incoming.at[off], out_send.at[off], out_recv.at[off], {"dp": to}))
    incoming[0] = outgoing[d]
    ranked[...] = grad_all.T.astype(BF16)

    for dt, ds in cross:
        ft, fs = behind(dt, ds)
        g = ft * n_s + fs
        k = dt * n_s + ds
        got = wfull.at[g, span(q_z, 0)]
        remote(got, got, wz_send.at[k, 0], wz_recv.at[k, 0], z_peer).wait_recv()
        go(remote(got, got, wd_send.at[k, 0], wd_recv.at[k, 0], y_peer))
        for c in range(2):
            got = wfull.at[g, span(q_y, c)]
            remote(got, got, wy_send.at[k, c], wy_recv.at[k, c], y_peer).wait_recv()
        go(remote(got, got, wd_send.at[k, 1], wd_recv.at[k, 1], z_peer))
    for c in range(2):
        at = pl.ds(c * half, half)
        for dt in range(1, n_t):
            ft = lax.rem(t - dt + n_t, n_t)
            got = dyfull.at[ft * n_s + s, at]
            remote(got, got, dx_send.at[dt, c], dx_recv.at[dt, c], {"tensor": ft}).wait_recv()
            go(remote(got, got, dc_send.at[dt, c], dc_recv.at[dt, c], core_peer))
    for c in range(2):
        at = pl.ds(c * half, half)
        for dt in range(1, n_t):
            got = dyfull.at[lax.rem(t - dt + n_t, n_t) * n_s + 1 - s, at]
            remote(got, got, dc_send.at[dt, c], dc_recv.at[dt, c], core_peer).wait_recv()

    def finish(q):
        @pl.loop(0, quarter // TILE)
        def _(j):
            at = pl.ds(pl.multiple_of(q * quarter + j * TILE, TILE), TILE)
            total = acc[:, at] + dot_nn(ranked[...], downs[:, :, at].reshape(n_dp * rk, TILE))
            for dt in range(1, n_t):
                for i in range(n_s):
                    g = lax.rem(t + dt, n_t) * n_s + i
                    total += dot_nt(dyfull[g], wfull[g, at])
            live_row = jnp.concatenate([keep_rows[...]] * (TILE // BLOCK), axis=1)
            out_ref[:, at] = jnp.where(live_row > 0, total, 0.0).astype(BF16)

    finish(q_own)
    for dt, ds in cross:
        ft, fs = behind(dt, ds)
        k = dt * n_s + ds
        got = wfull.at[ft * n_s + fs, span(q_z, 1)]
        remote(got, got, wz_send.at[k, 1], wz_recv.at[k, 1], z_peer).wait_recv()
    finish(q_z)
    finish(q_y)

    for off in range(1, n_dp):
        remote(outgoing.at[d], incoming.at[off], out_send.at[off], out_recv.at[off],
               {"dp": lax.rem(d - off + n_dp, n_dp)}).wait_recv()
    for j in range(local_slots):
        at = slice(j * RANK, (j + 1) * RANK)
        count = 0
        for tenant in range(tenants):
            count += jnp.where(slot_of[tenant] == d * local_slots + j, live_count[tenant], 0)
        sums = jnp.sum(incoming[:, at, :].astype(F32), 0)
        sums = sums / jnp.full((1, width + vl), count, jnp.int32).astype(F32)
        down_out[at, :] = sums[:, :width]
        up_out[at, :] = sums[:, width:]

    for dt, ds in cross:
        ft, fs = behind(dt, ds)
        g = ft * n_s + fs
        k = dt * n_s + ds
        for c, peer in enumerate((y_peer, z_peer)):
            got = wfull.at[g, span(q_yz, c)]
            remote(got, got, wd_send.at[k, c], wd_recv.at[k, c], peer).wait_recv()
    finish(q_yz)
    for copy in sent:
        copy.wait_send()


def body(x, dy, w, down_table, up_table, live_token_count, block_customer, customer_slot, dropout_flags):
    n_dp, n_t, n_s = (lax.axis_size(n) for n in ("dp", "tensor", "sub"))
    groups = n_t * n_s
    rows, width = x.shape
    vl = dy.shape[1]
    local_slots = down_table.shape[0]
    rk = local_slots * RANK
    all_rk = n_dp * rk
    vmem = pl.BlockSpec(memory_space=pltpu.VMEM)
    smem = pl.BlockSpec(memory_space=pltpu.SMEM)
    hbm = pl.BlockSpec(memory_space=pltpu.HBM)
    dma = pltpu.SemaphoreType.DMA
    input_grad, down_grad, up_grad = pl.pallas_call(
        functools.partial(kernel, (n_dp, n_t, n_s)),
        out_shape=(
            jax.ShapeDtypeStruct((rows, width), BF16),
            jax.ShapeDtypeStruct((rk, width), F32),
            jax.ShapeDtypeStruct((rk, vl), F32),
        ),
        in_specs=[hbm] * 5 + [smem] * 3 + [vmem],
        out_specs=(vmem, vmem, vmem),
        scratch_shapes=[
            pltpu.VMEM((rows, width), BF16),
            pltpu.VMEM((groups, width, vl), BF16),
            pltpu.VMEM((groups, rows, vl), BF16),
            pltpu.VMEM((rows, width), F32),
            pltpu.VMEM((n_dp, rk, width), BF16),
            pltpu.VMEM((n_dp, rk, vl), BF16),
            pltpu.VMEM((8, BLOCK), jnp.int32),
            pltpu.VMEM((n_dp, 8, BLOCK), jnp.int32),
            pltpu.VMEM((2 * RANK, rows), BF16),
            pltpu.VMEM((groups, 2 * RANK, rows), BF16),
            pltpu.VMEM((n_dp, rk, width + vl), BF16),
            pltpu.VMEM((n_dp, rk, width + vl), BF16),
            pltpu.VMEM((rows, BLOCK), F32),
            pltpu.VMEM((rows, all_rk), BF16),
            dma((5,)),
            dma((3, n_dp)), dma((3, n_dp)),
            dma((groups,)), dma((groups,)),
            dma((n_dp,)), dma((n_dp,)),
            dma((groups, 2)), dma((groups, 2)),
            dma((groups, 2)), dma((groups, 2)),
            dma((groups, 2)), dma((groups, 2)),
            dma((groups, 2)), dma((groups, 2)),
            dma, dma,
            dma((n_t, 2)), dma((n_t, 2)),
            dma((n_t, 2)), dma((n_t, 2)),
        ],
        compiler_params=pltpu.CompilerParams(
            collective_id=0, has_side_effects=True, vmem_limit_bytes=48 * 1024 * 1024
        ),
    )(x, dy, w, down_table.reshape(rk, width), up_table.reshape(rk, vl),
      live_token_count, block_customer, customer_slot, dropout_flags.reshape(1, -1))
    return input_grad, down_grad.reshape(local_slots, RANK, width), up_grad.reshape(local_slots, RANK, vl)


def solution(mesh):
    return jax.shard_map(
        body,
        mesh=mesh,
        in_specs=(
            P(("parts", "dp"), ("tensor", "sub")),
            P(("parts", "dp"), ("tensor", "sub")),
            P(None, ("tensor", "sub")),
            P(("parts", "dp"), None, ("tensor", "sub")),
            P(("parts", "dp"), None, ("tensor", "sub")),
            P("parts"),
            P(("parts", "dp")),
            P("parts"),
            P(("parts", "dp")),
        ),
        out_specs=(
            P(("parts", "dp"), ("tensor", "sub")),
            P(("parts", "dp"), None, ("tensor", "sub")),
            P(("parts", "dp"), None, ("tensor", "sub")),
        ),
        check_vma=False,
    )
```

time: 69.2 us -> 52.3 us (0.76)
  Pallas kernels: 56.3 us -> 42.8 us
  other arithmetic: 3.67 us -> 0 us
  local copies, waits for them, and re-layouts: 7.53 us -> 8.49 us
  between operations: 1.36 us -> 0.66 us
    pallas_call x2 -> x1, Pallas kernels: 56.3 us -> 42.8 us  [body(): pl.pallas_call(functools.partial(kernel, (n_dp, n_t, n_s)), out_shape=(ja...]
    unnamed x12 -> x17, local copies, waits for them, and re-layouts: 4.77 us -> 8.49 us
    reduce_sum x2 -> x0, other arithmetic: 1.41 us -> none  [the longest x1 0.78 us: body(): count = jnp.sum(onehot * live_token_count[None, :], 1)]
    div x2 -> x0, other arithmetic: 1.28 us -> none  [the longest x1 0.67 us: body(): sums[:, :, :width] / slot_count]
    shift_right_arithmetic x4 -> x0, local copies, waits for them, and re-layouts: 1.28 us -> none  [body(): jnp.right_shift(dropout_flags[None, :, None], shifts)]
    concatenate x1 -> x0, other arithmetic: 0.8 us -> none  [body(): jnp.concatenate([block_customer[1:] != block_customer[:-1], jnp.ones((1,)...]
    another operation x2 -> x0, local copies, waits for them, and re-layouts: 0.75 us -> none  [body(): meta = jnp.stack([slot, limit, block_customer] + [slot] * 5)]
where the time goes in v2:
time: 52.3 us; the launch traced here: 52 us
  Pallas kernels  42.8 us (82%)
  local copies, waits for them, and re-layouts  8.49 us (16%)
  between operations  0.66 us (1%)
    pallas_call x1, Pallas kernels, body(): pl.pallas_call(functools.partial(kernel, (n_dp, n_t, n_s)), out_shape=(ja...  42.8 us
    unnamed x17, local copies, waits for them, and re-layouts  8.49 us

profile of v2, /device:TPU:0, one launch (start us, length us, event | category | flops | bytes accessed | tf_op | source)
XLA Modules:
  0.0 52.0 jit_solution(12802319112121295727)
XLA Ops:
  0.6 0.0 copy-start
  0.6 1.0 %copy-done = bf16[1024,256]{1,0:T(8,128)(2,1)S(1)} copy-done((bf16[1024,256]{1,0:T(8,128)(2,1)S(1)}, bf16[1024,256]{1,0:T(8,128)(2,1)}, u32[]{:S(2)}) %copy-start) | copy-done | bytes 524312
  1.7 0.0 copy-start.1
  1.7 0.8 %copy-done.1 = bf16[1,16,2048]{2,1,0:T(8,128)(2,1)S(1)} copy-done((bf16[1,16,2048]{2,1,0:T(8,128)(2,1)S(1)}, bf16[1,16,2048]{2,1,0:T(8,128)(2,1)}, u32[]{:S(2)}) %copy-start.1) | copy-done | bytes 65560
  2.5 0.0 copy-start.2
  2.5 0.7 %copy-done.2 = bf16[1,16,256]{2,1,0:T(8,128)(2,1)S(1)} copy-done((bf16[1,16,256]{2,1,0:T(8,128)(2,1)S(1)}, bf16[1,16,256]{2,1,0:T(8,128)(2,1)}, u32[]{:S(2)}) %copy-start.2) | copy-done | bytes 8216
  3.2 0.0 copy-start.3
  3.2 0.7 %copy-done.3 = s32[512]{0:T(512)S(1)} copy-done((s32[512]{0:T(512)S(1)}, s32[512]{0:T(512)}, u32[]{:S(2)}) %copy-start.3) | copy-done | bytes 2072
  3.9 0.0 copy-start.4
  3.9 0.7 %copy-done.4 = s32[4]{0:T(128)S(1)} copy-done((s32[4]{0:T(128)S(1)}, s32[4]{0:T(128)}, u32[]{:S(2)}) %copy-start.4) | copy-done | bytes 40
  4.6 0.0 copy-start.5
  4.6 0.7 %copy-done.5 = s32[8]{0:T(128)S(1)} copy-done((s32[8]{0:T(128)S(1)}, s32[8]{0:T(128)}, u32[]{:S(2)}) %copy-start.5) | copy-done | bytes 56
  5.2 0.0 copy-start.6
  5.2 0.7 %copy-done.6 = s32[4]{0:T(128)S(1)} copy-done((s32[4]{0:T(128)S(1)}, s32[4]{0:T(128)}, u32[]{:S(2)}) %copy-start.6) | copy-done | bytes 40
  5.9 42.8 %shard_map.112 = (bf16[1024,2048]{1,0:T(8,128)(2,1)S(1)}, f32[16,2048]{1,0:T(8,128)S(1)}, f32[16,256]{1,0:T(8,128)S(1)}) custom-call(bf16[1024,2048]{1,0:T(8,128)(2,1)} %x_hbm.1, bf16[1024,256]{1,0:T(8,128)(2,1)S(1)} %copy-done, bf16[8192,256]{1,0:T(8,128)(2,1)} %w_hbm.1, bf16[16,2048]{1,0:T(8,128)(2,1)S(1)} %bitcast.6, bf16[16,256]{1,0:T(8,128)(2,1)S(1)} %bitcast.8, ...), custom_call_target="tpu_custom_call" | custom-call | tf_op jit(solution)/shard_map/pallas_call | solution.py:313
  48.7 2.0 %copy.15 = bf16[1024,2048]{1,0:T(8,128)(2,1)} copy(bf16[1024,2048]{1,0:T(8,128)(2,1)S(1)} %get-tuple-element.12) | data formatting | bytes 8388608
  50.7 0.7 %copy.16 = f32[1,16,2048]{2,1,0:T(8,128)} copy(f32[1,16,2048]{2,1,0:T(8,128)S(1)} %bitcast.5) | data formatting | bytes 262144
  51.3 0.6 %copy.17 = f32[1,16,256]{2,1,0:T(8,128)} copy(f32[1,16,256]{2,1,0:T(8,128)S(1)} %bitcast.7) | data formatting | bytes 32768
Async XLA Ops:
  0.6 1.0 %copy-start = (bf16[1024,256]{1,0:T(8,128)(2,1)S(1)}, bf16[1024,256]{1,0:T(8,128)(2,1)}, u32[]{:S(2)}) copy-start(bf16[1024,256]{1,0:T(8,128)(2,1)} %dy_hbm.1) | copy-start | bytes 1572868
  1.7 0.8 %copy-start.1 = (bf16[1,16,2048]{2,1,0:T(8,128)(2,1)S(1)}, bf16[1,16,2048]{2,1,0:T(8,128)(2,1)}, u32[]{:S(2)}) copy-start(bf16[1,16,2048]{2,1,0:T(8,128)(2,1)} %param.12) | copy-start | bytes 196612
  2.5 0.7 %copy-start.2 = (bf16[1,16,256]{2,1,0:T(8,128)(2,1)S(1)}, bf16[1,16,256]{2,1,0:T(8,128)(2,1)}, u32[]{:S(2)}) copy-start(bf16[1,16,256]{2,1,0:T(8,128)(2,1)} %param.13) | copy-start | bytes 24580
  3.2 0.7 %copy-start.3 = (s32[512]{0:T(512)S(1)}, s32[512]{0:T(512)}, u32[]{:S(2)}) copy-start(s32[512]{0:T(512)} %param.17) | copy-start | bytes 6148
  3.9 0.7 %copy-start.4 = (s32[4]{0:T(128)S(1)}, s32[4]{0:T(128)}, u32[]{:S(2)}) copy-start(s32[4]{0:T(128)} %live_count.1) | copy-start | bytes 52
  4.6 0.7 %copy-start.5 = (s32[8]{0:T(128)S(1)}, s32[8]{0:T(128)}, u32[]{:S(2)}) copy-start(s32[8]{0:T(128)} %customer.1) | copy-start | bytes 100
  5.2 0.7 %copy-start.6 = (s32[4]{0:T(128)S(1)}, s32[4]{0:T(128)}, u32[]{:S(2)}) copy-start(s32[4]{0:T(128)} %slot_of.1) | copy-start | bytes 52

commit v3 on v2

--- a/solution.py
+++ b/solution.py
@@ -11,9 +11,15 @@
 BLOCK = 128
 SCALE = 2.0
 TILE = 256
+PIECES = 4
+OVER_Y = 3
 MESH = pl.DeviceIdType.MESH
 F32 = jnp.float32
 BF16 = jnp.bfloat16
+
+
+def stay(array):
+    return pltpu.with_memory_space_constraint(array, pltpu.HBM)
 
 
 def dot_nt(a, b):
@@ -43,7 +49,7 @@
     blocks = rows // BLOCK
     tenants = live_count.shape[0]
     quarter = width // 4
-    piece = quarter // 2
+    piece = quarter // PIECES
     half = rows // 2
     odd = lax.rem(d, 2)
     z_peer = {"dp": d + 1 - 2 * odd}
@@ -129,7 +135,7 @@
     q_z = 2 * a + 1 - odd
     q_y = 2 * (1 - a) + odd
     q_yz = 2 * (1 - a) + 1 - odd
-    for c in range(2):
+    for c in range(PIECES):
         for dt, ds in cross:
             pt, ps = ahead(dt, ds)
             start = (pt * n_s + ps) * width + q_own * quarter + c * piece
@@ -144,7 +150,6 @@
             go(remote(dy_hbm.at[at], dyfull.at[me, at], dx_send.at[dt, c], dx_recv.at[dt, c],
                       {"tensor": lax.rem(t + dt, n_t)}))
 
-    send_dy(0)
     go(remote(dy_hbm, dyfull.at[me], dc_send.at[0, 0], dc_recv.at[0, 0], core_peer))
     other_rows = pl.ds(pl.multiple_of((t * n_s + 1 - s) * width, 16), width)
     go(remote(w_hbm.at[other_rows], wfull.at[me], wc_send, wc_recv, core_peer))
@@ -158,6 +163,8 @@
             go(remote(got, got, wz_send.at[k, c], wz_recv.at[k, c], z_peer))
             go(remote(got, got, wy_send.at[k, c], wy_recv.at[k, c], y_peer))
 
+    for c in range(PIECES // 2):
+        forward(c)
     for copy in own:
         copy.wait()
     for off in range(1, n_dp):
@@ -166,7 +173,6 @@
         remote(info, infos.at[off], tab_send.at[0, off], tab_recv.at[0, off], here).wait_recv()
         remote(up_hbm, ups.at[frm], tab_send.at[1, off], tab_recv.at[1, off], here).wait_recv()
         remote(down_hbm, downs.at[frm], tab_send.at[2, off], tab_recv.at[2, off], here).wait_recv()
-    forward(0)
     slots = n_dp * local_slots
     own_slot = lax.broadcasted_iota(jnp.int32, (slots, RANK, rows), 0) == slot_tok[None]
     in_all = dot_nt(downs[...].reshape(n_dp * rk, width), x_ref[...]).reshape(slots, RANK, rows)
@@ -177,7 +183,10 @@
         pt, ps = ahead(dt, ds)
         k = dt * n_s + ds
         go(remote(part, ranks.at[me], rk_send.at[k], rk_recv.at[k], {"tensor": pt, "sub": ps}))
-    send_dy(1)
+    for c in range(2):
+        send_dy(c)
+    for c in range(PIECES // 2, PIECES):
+        forward(c)
     ranks[me] = part[...]
 
     following = infos[n_dp - 1, 0:1, :]
@@ -192,7 +201,6 @@
         at = slice(b * BLOCK, (b + 1) * BLOCK)
         column = jnp.sum(jnp.where(eye, live[:, at], 0.0), 1, keepdims=True)
         keep_rows[at, :] = jnp.broadcast_to(column, (BLOCK, BLOCK))
-    forward(1)
 
     got = dyfull.at[t * n_s + 1 - s]
     remote(got, got, dc_send.at[0, 0], dc_recv.at[0, 0], core_peer).wait_recv()
@@ -232,46 +240,42 @@
         ft, fs = behind(dt, ds)
         g = ft * n_s + fs
         k = dt * n_s + ds
-        got = wfull.at[g, span(q_z, 0)]
-        remote(got, got, wz_send.at[k, 0], wz_recv.at[k, 0], z_peer).wait_recv()
-        go(remote(got, got, wd_send.at[k, 0], wd_recv.at[k, 0], y_peer))
-        for c in range(2):
-            got = wfull.at[g, span(q_y, c)]
-            remote(got, got, wy_send.at[k, c], wy_recv.at[k, c], y_peer).wait_recv()
-        go(remote(got, got, wd_send.at[k, 1], wd_recv.at[k, 1], z_peer))
-    for c in range(2):
+        for c in range(PIECES):
+            got_z = wfull.at[g, span(q_z, c)]
+            remote(got_z, got_z, wz_send.at[k, c], wz_recv.at[k, c], z_peer).wait_recv()
+            got_y = wfull.at[g, span(q_y, c)]
+            remote(got_y, got_y, wy_send.at[k, c], wy_recv.at[k, c], y_peer).wait_recv()
+            got, peer = (got_z, y_peer) if c < OVER_Y else (got_y, z_peer)
+            go(remote(got, got, wd_send.at[k, c], wd_recv.at[k, c], peer))
+
+    def pass_on(c):
         at = pl.ds(c * half, half)
         for dt in range(1, n_t):
             ft = lax.rem(t - dt + n_t, n_t)
             got = dyfull.at[ft * n_s + s, at]
             remote(got, got, dx_send.at[dt, c], dx_recv.at[dt, c], {"tensor": ft}).wait_recv()
             go(remote(got, got, dc_send.at[dt, c], dc_recv.at[dt, c], core_peer))
-    for c in range(2):
-        at = pl.ds(c * half, half)
         for dt in range(1, n_t):
             got = dyfull.at[lax.rem(t - dt + n_t, n_t) * n_s + 1 - s, at]
             remote(got, got, dc_send.at[dt, c], dc_recv.at[dt, c], core_peer).wait_recv()
 
-    def finish(q):
+    def finish(c, q):
+        high = pl.ds(c * half, half)
+
         @pl.loop(0, quarter // TILE)
         def _(j):
             at = pl.ds(pl.multiple_of(q * quarter + j * TILE, TILE), TILE)
-            total = acc[:, at] + dot_nn(ranked[...], downs[:, :, at].reshape(n_dp * rk, TILE))
+            total = acc[high, at] + dot_nn(ranked[high, :], downs[:, :, at].reshape(n_dp * rk, TILE))
             for dt in range(1, n_t):
                 for i in range(n_s):
                     g = lax.rem(t + dt, n_t) * n_s + i
-                    total += dot_nt(dyfull[g], wfull[g, at])
-            live_row = jnp.concatenate([keep_rows[...]] * (TILE // BLOCK), axis=1)
-            out_ref[:, at] = jnp.where(live_row > 0, total, 0.0).astype(BF16)
-
-    finish(q_own)
-    for dt, ds in cross:
-        ft, fs = behind(dt, ds)
-        k = dt * n_s + ds
-        got = wfull.at[ft * n_s + fs, span(q_z, 1)]
-        remote(got, got, wz_send.at[k, 1], wz_recv.at[k, 1], z_peer).wait_recv()
-    finish(q_z)
-    finish(q_y)
+                    total += dot_nt(dyfull[g, high, :], wfull[g, at])
+            live_row = jnp.concatenate([keep_rows[high, :]] * (TILE // BLOCK), axis=1)
+            out_ref[high, at] = jnp.where(live_row > 0, total, 0.0).astype(BF16)
+
+    pass_on(0)
+    for q in (q_own, q_z, q_y):
+        finish(0, q)
 
     for off in range(1, n_dp):
         remote(outgoing.at[d], incoming.at[off], out_send.at[off], out_recv.at[off],
@@ -290,10 +294,13 @@
         ft, fs = behind(dt, ds)
         g = ft * n_s + fs
         k = dt * n_s + ds
-        for c, peer in enumerate((y_peer, z_peer)):
+        for c in range(PIECES):
             got = wfull.at[g, span(q_yz, c)]
-            remote(got, got, wd_send.at[k, c], wd_recv.at[k, c], peer).wait_recv()
-    finish(q_yz)
+            remote(got, got, wd_send.at[k, c], wd_recv.at[k, c], y_peer if c < OVER_Y else z_peer).wait_recv()
+    finish(0, q_yz)
+    pass_on(1)
+    for q in (q_own, q_z, q_y, q_yz):
+        finish(1, q)
     for copy in sent:
         copy.wait_send()
 
@@ -338,10 +345,10 @@
             dma((3, n_dp)), dma((3, n_dp)),
             dma((groups,)), dma((groups,)),
             dma((n_dp,)), dma((n_dp,)),
-            dma((groups, 2)), dma((groups, 2)),
-            dma((groups, 2)), dma((groups, 2)),
-            dma((groups, 2)), dma((groups, 2)),
-            dma((groups, 2)), dma((groups, 2)),
+            dma((groups, PIECES)), dma((groups, PIECES)),
+            dma((groups, PIECES)), dma((groups, PIECES)),
+            dma((groups, PIECES)), dma((groups, PIECES)),
+            dma((groups, PIECES)), dma((groups, PIECES)),
             dma, dma,
             dma((n_t, 2)), dma((n_t, 2)),
             dma((n_t, 2)), dma((n_t, 2)),
@@ -349,8 +356,8 @@
         compiler_params=pltpu.CompilerParams(
             collective_id=0, has_side_effects=True, vmem_limit_bytes=48 * 1024 * 1024
         ),
-    )(x, dy, w, down_table.reshape(rk, width), up_table.reshape(rk, vl),
-      live_token_count, block_customer, customer_slot, dropout_flags.reshape(1, -1))
+    )(x, stay(dy), w, stay(down_table.reshape(rk, width)), stay(up_table.reshape(rk, vl)),
+      stay(live_token_count), stay(block_customer), stay(customer_slot), stay(dropout_flags.reshape(1, -1)))
     return input_grad, down_grad.reshape(local_slots, RANK, width), up_grad.reshape(local_slots, RANK, vl)
 
 

time: 52.3 us -> 45.7 us (0.87)
  local copies, waits for them, and re-layouts: 8.49 us -> 3.28 us
  Pallas kernels: 42.8 us -> 41.6 us
    unnamed x17 -> x3, local copies, waits for them, and re-layouts: 8.49 us -> 3.28 us
    pallas_call x1, Pallas kernels: 42.8 us -> 41.6 us  [body(): pl.pallas_call(functools.partial(kernel, (n_dp, n_t, n_s)), out_shape=(ja...]
where the time goes in v3:
time: 45.7 us; the launch traced here: 45.5 us
  Pallas kernels  41.6 us (91%)
  local copies, waits for them, and re-layouts  3.28 us (7%)
  between operations  0.64 us (1%)
    pallas_call x1, Pallas kernels, body(): pl.pallas_call(functools.partial(kernel, (n_dp, n_t, n_s)), out_shape=(ja...  41.6 us
    unnamed x3, local copies, waits for them, and re-layouts  3.28 us

profile of v3, /device:TPU:0, one launch (start us, length us, event | category | flops | bytes accessed | tf_op | source)
XLA Modules:
  0.0 45.5 jit_solution(7180162973645554993)
XLA Ops:
  0.6 41.6 %shard_map.112 = (bf16[1024,2048]{1,0:T(8,128)(2,1)S(1)}, f32[16,2048]{1,0:T(8,128)S(1)}, f32[16,256]{1,0:T(8,128)S(1)}) custom-call(bf16[1024,2048]{1,0:T(8,128)(2,1)} %x_hbm.1, bf16[1024,256]{1,0:T(8,128)(2,1)} %dy_hbm.1, bf16[8192,256]{1,0:T(8,128)(2,1)} %w_hbm.1, bf16[16,2048]{1,0:T(8,128)(2,1)} %bitcast.7, bf16[16,256]{1,0:T(8,128)(2,1)} %bitcast.8, ...), custom_call_target="tpu_custom_call" | custom-call | tf_op jit(solution)/shard_map/pallas_call | solution.py:320
  42.3 2.0 %copy.15 = bf16[1024,2048]{1,0:T(8,128)(2,1)} copy(bf16[1024,2048]{1,0:T(8,128)(2,1)S(1)} %get-tuple-element.12) | data formatting | bytes 8388608
  44.3 0.7 %copy.16 = f32[1,16,2048]{2,1,0:T(8,128)} copy(f32[1,16,2048]{2,1,0:T(8,128)S(1)} %bitcast.5) | data formatting | bytes 262144
  44.9 0.6 %copy.17 = f32[1,16,256]{2,1,0:T(8,128)} copy(f32[1,16,256]{2,1,0:T(8,128)S(1)} %bitcast.6) | data formatting | bytes 32768

commit v4 on v3

--- a/solution.py
+++ b/solution.py
@@ -10,9 +10,9 @@
 RANK = 16
 BLOCK = 128
 SCALE = 2.0
-TILE = 256
 PIECES = 4
 OVER_Y = 3
+STAGES = ((0, 2), (2, 3), (3, 4))
 MESH = pl.DeviceIdType.MESH
 F32 = jnp.float32
 BF16 = jnp.bfloat16
@@ -43,14 +43,14 @@
     a, d, t, s = (lax.axis_index(n) for n in ("parts", "dp", "tensor", "sub"))
     me = t * n_s + s
     rows, width = x_ref.shape
-    vl = dyfull.shape[2]
+    vl = up_hbm.shape[1]
     rk = down_hbm.shape[0]
     local_slots = rk // RANK
     blocks = rows // BLOCK
     tenants = live_count.shape[0]
     quarter = width // 4
     piece = quarter // PIECES
-    half = rows // 2
+    share = rows // PIECES
     odd = lax.rem(d, 2)
     z_peer = {"dp": d + 1 - 2 * odd}
     y_peer = {"parts": 1 - a}
@@ -61,6 +61,12 @@
 
     def behind(dt, ds):
         return lax.rem(t - dt + n_t, n_t), lax.rem(s - ds + n_s, n_s)
+
+    def cols(g):
+        return pl.ds(pl.multiple_of(g * vl, BLOCK), vl)
+
+    def chip_cols(tt):
+        return pl.ds(pl.multiple_of(tt * n_s * vl, BLOCK), n_s * vl)
 
     group = [(dt, ds) for dt in range(n_t) for ds in range(n_s) if (dt, ds) != (0, 0)]
     cross = [(dt, ds) for dt, ds in group if dt]
@@ -83,9 +89,9 @@
     own = [
         pltpu.make_async_copy(down_hbm, downs.at[d], own_sem.at[0]),
         pltpu.make_async_copy(up_hbm, ups.at[d], own_sem.at[1]),
-        pltpu.make_async_copy(dy_hbm, dyfull.at[me], own_sem.at[2]),
+        pltpu.make_async_copy(dy_hbm, dyfull.at[:, cols(me)], own_sem.at[2]),
         pltpu.make_async_copy(x_hbm, x_ref, own_sem.at[3]),
-        pltpu.make_async_copy(w_hbm.at[own_rows], wfull.at[me], own_sem.at[4]),
+        pltpu.make_async_copy(w_hbm.at[own_rows], wfull.at[:, cols(me)], own_sem.at[4]),
     ]
     for copy in own:
         copy.start()
@@ -141,24 +147,24 @@
             start = (pt * n_s + ps) * width + q_own * quarter + c * piece
             src = w_hbm.at[pl.ds(pl.multiple_of(start, 16), piece)]
             k = dt * n_s + ds
-            go(remote(src, wfull.at[me, span(q_own, c)], wx_send.at[k, c], wx_recv.at[k, c],
+            go(remote(src, wfull.at[span(q_own, c), cols(me)], wx_send.at[k, c], wx_recv.at[k, c],
                       {"tensor": pt, "sub": ps}))
 
     def send_dy(c):
-        at = pl.ds(c * half, half)
+        at = pl.ds(c * share, share)
         for dt in range(1, n_t):
-            go(remote(dy_hbm.at[at], dyfull.at[me, at], dx_send.at[dt, c], dx_recv.at[dt, c],
+            go(remote(dy_hbm.at[at], dyfull.at[at, cols(me)], dx_send.at[dt, c], dx_recv.at[dt, c],
                       {"tensor": lax.rem(t + dt, n_t)}))
 
-    go(remote(dy_hbm, dyfull.at[me], dc_send.at[0, 0], dc_recv.at[0, 0], core_peer))
+    go(remote(dy_hbm, dyfull.at[:, cols(me)], dc_send.at[0, 0], dc_recv.at[0, 0], core_peer))
     other_rows = pl.ds(pl.multiple_of((t * n_s + 1 - s) * width, 16), width)
-    go(remote(w_hbm.at[other_rows], wfull.at[me], wc_send, wc_recv, core_peer))
+    go(remote(w_hbm.at[other_rows], wfull.at[:, cols(me)], wc_send, wc_recv, core_peer))
 
     def forward(c):
         for dt, ds in cross:
             ft, fs = behind(dt, ds)
             k = dt * n_s + ds
-            got = wfull.at[ft * n_s + fs, span(q_own, c)]
+            got = wfull.at[span(q_own, c), cols(ft * n_s + fs)]
             remote(got, got, wx_send.at[k, c], wx_recv.at[k, c], {"tensor": ft, "sub": fs}).wait_recv()
             go(remote(got, got, wz_send.at[k, c], wz_recv.at[k, c], z_peer))
             go(remote(got, got, wy_send.at[k, c], wy_recv.at[k, c], y_peer))
@@ -176,14 +182,14 @@
     slots = n_dp * local_slots
     own_slot = lax.broadcasted_iota(jnp.int32, (slots, RANK, rows), 0) == slot_tok[None]
     in_all = dot_nt(downs[...].reshape(n_dp * rk, width), x_ref[...]).reshape(slots, RANK, rows)
-    grad_all = dot_nt(ups[...].reshape(n_dp * rk, vl), dyfull[me]).reshape(slots, RANK, rows)
+    grad_all = dot_nt(ups[...].reshape(n_dp * rk, vl), dyfull[:, cols(me)]).reshape(slots, RANK, rows)
     part[0:RANK, :] = jnp.sum(jnp.where(own_slot, in_all, 0.0), 0).astype(BF16)
     part[RANK:2 * RANK, :] = jnp.sum(jnp.where(own_slot, grad_all, 0.0), 0).astype(BF16)
     for dt, ds in group:
         pt, ps = ahead(dt, ds)
         k = dt * n_s + ds
         go(remote(part, ranks.at[me], rk_send.at[k], rk_recv.at[k], {"tensor": pt, "sub": ps}))
-    for c in range(2):
+    for c in range(PIECES):
         send_dy(c)
     for c in range(PIECES // 2, PIECES):
         forward(c)
@@ -202,18 +208,30 @@
         column = jnp.sum(jnp.where(eye, live[:, at], 0.0), 1, keepdims=True)
         keep_rows[at, :] = jnp.broadcast_to(column, (BLOCK, BLOCK))
 
-    got = dyfull.at[t * n_s + 1 - s]
+    def forward_far(c):
+        for dt, ds in cross:
+            ft, fs = behind(dt, ds)
+            g = ft * n_s + fs
+            k = dt * n_s + ds
+            got_z = wfull.at[span(q_z, c), cols(g)]
+            remote(got_z, got_z, wz_send.at[k, c], wz_recv.at[k, c], z_peer).wait_recv()
+            got_y = wfull.at[span(q_y, c), cols(g)]
+            remote(got_y, got_y, wy_send.at[k, c], wy_recv.at[k, c], y_peer).wait_recv()
+            got, peer = (got_z, y_peer) if c < OVER_Y else (got_y, z_peer)
+            go(remote(got, got, wd_send.at[k, c], wd_recv.at[k, c], peer))
+
+    for c in range(PIECES // 2):
+        forward_far(c)
+
+    got = dyfull.at[:, cols(t * n_s + 1 - s)]
     remote(got, got, dc_send.at[0, 0], dc_recv.at[0, 0], core_peer).wait_recv()
-    got = wfull.at[t * n_s + 1 - s]
+    got = wfull.at[:, cols(t * n_s + 1 - s)]
     remote(got, got, wc_send, wc_recv, core_peer).wait_recv()
 
-    @pl.loop(0, width // TILE)
+    @pl.loop(0, 4)
     def _(j):
-        at = pl.ds(pl.multiple_of(j * TILE, TILE), TILE)
-        total = dot_nt(dyfull[t * n_s], wfull[t * n_s, at])
-        for i in range(1, n_s):
-            total += dot_nt(dyfull[t * n_s + i], wfull[t * n_s + i, at])
-        acc[:, at] = total
+        at = pl.ds(pl.multiple_of(j * quarter, quarter), quarter)
+        acc[:, at] = dot_nt(dyfull[:, chip_cols(t)], wfull[at, chip_cols(t)])
 
     for dt, ds in group:
         ft, fs = behind(dt, ds)
@@ -226,7 +244,7 @@
     grad_rank = total[RANK:2 * RANK] * keep
     dropped_all = jnp.where(own_slot, dropped[None], 0.0).reshape(n_dp * rk, rows).astype(BF16)
     grad_all = jnp.where(own_slot, grad_rank[None], 0.0).reshape(n_dp * rk, rows)
-    up_part = dot_nn(dropped_all, dyfull[me])
+    up_part = dot_nn(dropped_all, dyfull[:, cols(me)])
     outgoing[:, :, width:] = up_part.reshape(n_dp, rk, vl).astype(BF16)
     down_part = dot_nn(grad_all.astype(BF16), x_ref[...])
     outgoing[:, :, :width] = down_part.reshape(n_dp, rk, width).astype(BF16)
@@ -236,47 +254,58 @@
     incoming[0] = outgoing[d]
     ranked[...] = grad_all.T.astype(BF16)
 
+    for c in range(PIECES // 2, PIECES):
+        forward_far(c)
+
+    def pass_on(c):
+        at = pl.ds(c * share, share)
+        for dt in range(1, n_t):
+            ft = lax.rem(t - dt + n_t, n_t)
+            got = dyfull.at[at, cols(ft * n_s + s)]
+            remote(got, got, dx_send.at[dt, c], dx_recv.at[dt, c], {"tensor": ft}).wait_recv()
+            go(remote(got, got, dc_send.at[dt, c], dc_recv.at[dt, c], core_peer))
+        for dt in range(1, n_t):
+            got = dyfull.at[at, cols(lax.rem(t - dt + n_t, n_t) * n_s + 1 - s)]
+            remote(got, got, dc_send.at[dt, c], dc_recv.at[dt, c], core_peer).wait_recv()
+
+    @pl.loop(0, 4)
+    def _(j):
+        at = pl.ds(pl.multiple_of(j * quarter, quarter), quarter)
+        acc[:, at] += dot_nn(ranked[...], downs[:, :, at].reshape(n_dp * rk, quarter))
+
+    def finish(stage, q):
+        first, end = STAGES[stage]
+        high = pl.ds(first * share, (end - first) * share)
+        at = pl.ds(pl.multiple_of(q * quarter, quarter), quarter)
+        total = acc[high, at]
+        for dt in range(1, n_t):
+            far = chip_cols(lax.rem(t + dt, n_t))
+            total += dot_nt(dyfull[high, far], wfull[at, far])
+        live_row = jnp.concatenate([keep_rows[high, :]] * (quarter // BLOCK), axis=1)
+        out_ref[high, at] = jnp.where(live_row > 0, total, 0.0).astype(BF16)
+
+    def finish_all(stage):
+        @pl.loop(0, 4)
+        def _(q):
+            finish(stage, q)
+
+    for c in range(*STAGES[0]):
+        pass_on(c)
+    for q in (q_own, q_z, q_y):
+        finish(0, q)
+
     for dt, ds in cross:
         ft, fs = behind(dt, ds)
         g = ft * n_s + fs
         k = dt * n_s + ds
         for c in range(PIECES):
-            got_z = wfull.at[g, span(q_z, c)]
-            remote(got_z, got_z, wz_send.at[k, c], wz_recv.at[k, c], z_peer).wait_recv()
-            got_y = wfull.at[g, span(q_y, c)]
-            remote(got_y, got_y, wy_send.at[k, c], wy_recv.at[k, c], y_peer).wait_recv()
-            got, peer = (got_z, y_peer) if c < OVER_Y else (got_y, z_peer)
-            go(remote(got, got, wd_send.at[k, c], wd_recv.at[k, c], peer))
-
-    def pass_on(c):
-        at = pl.ds(c * half, half)
-        for dt in range(1, n_t):
-            ft = lax.rem(t - dt + n_t, n_t)
-            got = dyfull.at[ft * n_s + s, at]
-            remote(got, got, dx_send.at[dt, c], dx_recv.at[dt, c], {"tensor": ft}).wait_recv()
-            go(remote(got, got, dc_send.at[dt, c], dc_recv.at[dt, c], core_peer))
-        for dt in range(1, n_t):
-            got = dyfull.at[lax.rem(t - dt + n_t, n_t) * n_s + 1 - s, at]
-            remote(got, got, dc_send.at[dt, c], dc_recv.at[dt, c], core_peer).wait_recv()
-
-    def finish(c, q):
-        high = pl.ds(c * half, half)
-
-        @pl.loop(0, quarter // TILE)
-        def _(j):
-            at = pl.ds(pl.multiple_of(q * quarter + j * TILE, TILE), TILE)
-            total = acc[high, at] + dot_nn(ranked[high, :], downs[:, :, at].reshape(n_dp * rk, TILE))
-            for dt in range(1, n_t):
-                for i in range(n_s):
-                    g = lax.rem(t + dt, n_t) * n_s + i
-                    total += dot_nt(dyfull[g, high, :], wfull[g, at])
-            live_row = jnp.concatenate([keep_rows[high, :]] * (TILE // BLOCK), axis=1)
-            out_ref[high, at] = jnp.where(live_row > 0, total, 0.0).astype(BF16)
-
-    pass_on(0)
-    for q in (q_own, q_z, q_y):
-        finish(0, q)
-
+            got = wfull.at[span(q_yz, c), cols(g)]
+            remote(got, got, wd_send.at[k, c], wd_recv.at[k, c], y_peer if c < OVER_Y else z_peer).wait_recv()
+    finish(0, q_yz)
+    for stage in range(1, len(STAGES)):
+        for c in range(*STAGES[stage]):
+            pass_on(c)
+        finish_all(stage)
     for off in range(1, n_dp):
         remote(outgoing.at[d], incoming.at[off], out_send.at[off], out_recv.at[off],
                {"dp": lax.rem(d - off + n_dp, n_dp)}).wait_recv()
@@ -289,18 +318,6 @@
         sums = sums / jnp.full((1, width + vl), count, jnp.int32).astype(F32)
         down_out[at, :] = sums[:, :width]
         up_out[at, :] = sums[:, width:]
-
-    for dt, ds in cross:
-        ft, fs = behind(dt, ds)
-        g = ft * n_s + fs
-        k = dt * n_s + ds
-        for c in range(PIECES):
-            got = wfull.at[g, span(q_yz, c)]
-            remote(got, got, wd_send.at[k, c], wd_recv.at[k, c], y_peer if c < OVER_Y else z_peer).wait_recv()
-    finish(0, q_yz)
-    pass_on(1)
-    for q in (q_own, q_z, q_y, q_yz):
-        finish(1, q)
     for copy in sent:
         copy.wait_send()
 
@@ -328,8 +345,8 @@
         out_specs=(vmem, vmem, vmem),
         scratch_shapes=[
             pltpu.VMEM((rows, width), BF16),
-            pltpu.VMEM((groups, width, vl), BF16),
-            pltpu.VMEM((groups, rows, vl), BF16),
+            pltpu.VMEM((width, groups * vl), BF16),
+            pltpu.VMEM((rows, groups * vl), BF16),
             pltpu.VMEM((rows, width), F32),
             pltpu.VMEM((n_dp, rk, width), BF16),
             pltpu.VMEM((n_dp, rk, vl), BF16),
@@ -350,8 +367,8 @@
             dma((groups, PIECES)), dma((groups, PIECES)),
             dma((groups, PIECES)), dma((groups, PIECES)),
             dma, dma,
-            dma((n_t, 2)), dma((n_t, 2)),
-            dma((n_t, 2)), dma((n_t, 2)),
+            dma((n_t, PIECES)), dma((n_t, PIECES)),
+            dma((n_t, PIECES)), dma((n_t, PIECES)),
         ],
         compiler_params=pltpu.CompilerParams(
             collective_id=0, has_side_effects=True, vmem_limit_bytes=48 * 1024 * 1024

time: 45.7 us -> 44.3 us (0.969)
  Pallas kernels: 41.6 us -> 40.2 us
    pallas_call x1, Pallas kernels: 41.6 us -> 40.2 us  [body(): pl.pallas_call(functools.partial(kernel, (n_dp, n_t, n_s)), out_shape=(ja...]
where the time goes in v4:
time: 44.3 us; the launch traced here: 44.1 us
  Pallas kernels  40.2 us (91%)
  local copies, waits for them, and re-layouts  3.28 us (7%)
  between operations  0.64 us (1%)
    pallas_call x1, Pallas kernels, body(): pl.pallas_call(functools.partial(kernel, (n_dp, n_t, n_s)), out_shape=(ja...  40.2 us
    unnamed x3, local copies, waits for them, and re-layouts  3.28 us

profile of v4, /device:TPU:0, one launch (start us, length us, event | category | flops | bytes accessed | tf_op | source)
XLA Modules:
  0.0 44.1 jit_solution(8814106125201747930)
XLA Ops:
  0.6 40.2 %shard_map.112 = (bf16[1024,2048]{1,0:T(8,128)(2,1)S(1)}, f32[16,2048]{1,0:T(8,128)S(1)}, f32[16,256]{1,0:T(8,128)S(1)}) custom-call(bf16[1024,2048]{1,0:T(8,128)(2,1)} %x_hbm.1, bf16[1024,256]{1,0:T(8,128)(2,1)} %dy_hbm.1, bf16[8192,256]{1,0:T(8,128)(2,1)} %w_hbm.1, bf16[16,2048]{1,0:T(8,128)(2,1)} %bitcast.7, bf16[16,256]{1,0:T(8,128)(2,1)} %bitcast.8, ...), custom_call_target="tpu_custom_call" | custom-call | tf_op jit(solution)/shard_map/pallas_call | solution.py:337
  40.9 2.0 %copy.15 = bf16[1024,2048]{1,0:T(8,128)(2,1)} copy(bf16[1024,2048]{1,0:T(8,128)(2,1)S(1)} %get-tuple-element.12) | data formatting | bytes 8388608
  42.9 0.7 %copy.16 = f32[1,16,2048]{2,1,0:T(8,128)} copy(f32[1,16,2048]{2,1,0:T(8,128)S(1)} %bitcast.5) | data formatting | bytes 262144
  43.5 0.6 %copy.17 = f32[1,16,256]{2,1,0:T(8,128)} copy(f32[1,16,256]{2,1,0:T(8,128)S(1)} %bitcast.6) | data formatting | bytes 32768
